TPU v7x, 128 devices: a whole 4x4x4 slice. The times are simulated.
128 devices in a mesh: sec: 2 (over x_lo), head: 8 (over z, x_hi), seq: 8 (over y, core).
Axes of the slice: x: 4 (x_hi: 2, x_lo: 2; x = x_hi * 2 + x_lo), y: 4, z: 4, core: 2. Of those that a mesh axis runs over, the one named last changes fastest.
Arguments:
- inputs: bfloat16 [8, 2048, 4096], P('seq', 'sec'), may hold values from -16 to 16
- w_query: bfloat16 [4096, 4096], P(None, 'head'), may hold values from -0.09375 to 0.09375
- w_key: bfloat16 [4096, 1024], P(None, 'head'), may hold values from -0.09375 to 0.09375
- teacher_queries: bfloat16 [8, 2048, 16384], P('seq', 'head', 'sec'), may hold values from -256 to 256
- teacher_keys: bfloat16 [8, 2048, 16384], P('seq', 'head', 'sec'), may hold values from -8 to 8
- head_match: int32 [32], replicated, may hold values from 0 to 127, as said below
- block_order: int32 [16], replicated, may hold values from 0 to 15, each once
Outputs:
- grad_inputs: bfloat16 [8, 2048, 4096], P('seq', ('sec', 'head'))
- grad_query: bfloat16 [4096, 4096], P(('sec', 'seq'), 'head')
- grad_key: bfloat16 [4096, 1024], P(('sec', 'seq'), 'head')
Inputs may be any that keep to these rules, and one draw needn't show every extreme that they name: `head_match`: entries may repeat. Split the teacher heads into 2 aligned sections of 64: heads s * 64 to (s + 1) * 64 - 1. Within each aligned block of 4 entries starting at entry 0, at most 2 distinct teacher heads lie in each aligned section, and some run of entries has exactly 2 distinct ones in section 0. `block_order`: each block index once.
All inputs are finite; a program needn't handle non-finite values.
Results may differ from a plain program's by a relative error of at most 0.025.
Values may be sent and summed in bfloat16 or wider, within the bound.
A program may use at most 128 MiB of HBM per device.

v0:
```python
import math

import jax
import jax.numpy as jnp
from jax import lax
from jax.sharding import PartitionSpec as P

HD = 128
QB = 128


rope_base = 500000.0
grad_scale = 16.0


def positions_of(block_order):
    offsets = jnp.arange(QB, dtype=jnp.int32)
    return (block_order[:, None] * QB + offsets[None, :]).reshape(-1)


def rope_tables(positions):
    half = HD // 2
    freqs = rope_base ** (-(jnp.arange(half, dtype=jnp.float32) * 2.0) / HD)
    angles = positions.astype(jnp.float32)[:, None] * freqs[None, :]
    return (jnp.cos(angles), jnp.sin(angles))


def rotate(values, cosine, sine):
    half = values.shape[-1] // 2
    first = values[..., :half]
    second = values[..., half:]
    return jnp.concatenate(
        [first * cosine - second * sine, second * cosine + first * sine], axis=-1
    )


def rotate_back(grads, cosine, sine):
    half = grads.shape[-1] // 2
    first = grads[..., :half]
    second = grads[..., half:]
    return jnp.concatenate(
        [first * cosine + second * sine, second * cosine - first * sine], axis=-1
    )


def masked_softmax(scores, visible):
    masked = jnp.where(visible, scores, -jnp.inf)
    top = jnp.max(masked, axis=-1, keepdims=True)
    weights = jnp.where(visible, jnp.exp(masked - top), 0.0)
    return weights / jnp.sum(weights, axis=-1, keepdims=True)


def shards(inputs, w_query, w_key, teacher_queries, teacher_keys, head_match, block_order):
    sec_count = lax.axis_size("sec")
    head_count = lax.axis_size("head")
    sec_index = lax.axis_index("sec")
    head_index = lax.axis_index("head")
    scale = 1.0 / math.sqrt(HD)
    tokens = inputs[0]
    rows = tokens.shape[0]
    length = rows * sec_count
    heads_dev = w_query.shape[1] // HD
    kv_dev = w_key.shape[1] // HD
    group = heads_dev // kv_dev
    trows = teacher_queries.shape[1]
    sect_heads = teacher_queries.shape[2] // HD
    positions = positions_of(block_order)
    cosine, sine = rope_tables(positions)
    own_positions = lax.dynamic_slice_in_dim(positions, sec_index * rows, rows, 0)
    own_cos = lax.dynamic_slice_in_dim(cosine, sec_index * rows, rows, 0)
    own_sin = lax.dynamic_slice_in_dim(sine, sec_index * rows, rows, 0)
    visible = positions[None, :] <= own_positions[:, None]
    queries = (
        jnp.dot(tokens, w_query, preferred_element_type=jnp.float32)
        .reshape(rows, heads_dev, HD)
        .transpose(1, 0, 2)
    )
    queries = rotate(queries, own_cos, own_sin).astype(jnp.bfloat16)
    own_keys = (
        jnp.dot(tokens, w_key, preferred_element_type=jnp.float32)
        .reshape(rows, kv_dev, HD)
        .transpose(1, 0, 2)
    )
    own_keys = rotate(own_keys, own_cos, own_sin).astype(jnp.bfloat16)
    all_keys = lax.all_gather(own_keys, "sec", axis=1, tiled=True)
    match_rows = head_match.reshape(head_count, heads_dev)
    local_q = teacher_queries[0].reshape(trows, sect_heads, HD)
    local_k = teacher_keys[0].reshape(trows, sect_heads, HD)
    own_half = head_index // (head_count // sec_count)
    mine = lax.dynamic_index_in_dim(match_rows, head_index, 0, keepdims=False)
    sections = mine // sect_heads
    valid = match_rows // sect_heads == sec_index
    slots = match_rows.shape[1]
    local = jnp.clip(match_rows - sec_index * sect_heads, 0, sect_heads - 1).reshape(-1)
    keep = valid.reshape(-1)[:, None, None]
    picked_q = jnp.take(local_q, local, axis=1).transpose(1, 0, 2)
    picked_k = jnp.take(local_k, local, axis=1).transpose(1, 0, 2)
    picked_q = jnp.where(keep, picked_q, jnp.zeros_like(picked_q))
    picked_k = jnp.where(keep, picked_k, jnp.zeros_like(picked_k))
    to_half = (jnp.arange(sec_count) == own_half)[:, None, None, None]
    send_q = jnp.where(to_half, picked_q[None], jnp.zeros_like(picked_q)[None])
    send_k = jnp.broadcast_to(picked_k[None], (sec_count,) + picked_k.shape)
    full_shape = (sec_count * head_count, slots, trows, HD)
    sent_q = send_q.reshape(full_shape)
    sent_k = send_k.reshape(full_shape)
    got_q, got_k = (
        lax.all_to_all(sent_q, ("sec", "head"), split_axis=0, concat_axis=0, tiled=True),
        lax.all_to_all(sent_k, ("sec", "head"), split_axis=0, concat_axis=0, tiled=True),
    )
    slot_of = jnp.arange(heads_dev, dtype=jnp.int32)
    slots_sent = got_q.shape[1]
    blocks_q = got_q.reshape(sec_count, head_count, slots_sent, trows, HD)[sections, :, slot_of]
    blocks_k = got_k.reshape(sec_count, head_count, slots_sent, trows, HD)[sections, :, slot_of]
    teacher_q = lax.dynamic_slice_in_dim(
        blocks_q.reshape(heads_dev, length, HD), sec_index * rows, rows, 1
    )
    teacher_k = blocks_k.reshape(heads_dev, length, HD)

    def one_head(key_total, head_data):
        query, t_query, t_key, which = head_data
        kv_group = which // group
        key_one = lax.dynamic_index_in_dim(all_keys, kv_group, 0, keepdims=False)
        contract = (((1,), (1,)), ((), ()))
        student = (
            lax.dot_general(query, key_one, contract, preferred_element_type=jnp.float32) * scale
        )
        teacher = (
            lax.dot_general(t_query, t_key, contract, preferred_element_type=jnp.float32) * scale
        )
        p_student = masked_softmax(student, visible)
        p_teacher = masked_softmax(teacher, visible)
        score_grads = ((p_student - p_teacher) * grad_scale).astype(jnp.bfloat16)
        query_grads = jnp.dot(score_grads, key_one, preferred_element_type=jnp.float32) * scale
        query_grads = rotate_back(query_grads, own_cos, own_sin).astype(jnp.bfloat16)
        key_term = (
            lax.dot_general(
                score_grads, query, (((0,), (0,)), ((), ())), preferred_element_type=jnp.float32
            )
            * scale
        )
        current = lax.dynamic_index_in_dim(key_total, kv_group, 0, keepdims=False)
        key_total = lax.dynamic_update_index_in_dim(key_total, current + key_term, kv_group, 0)
        return (key_total, query_grads)

    key_start = jnp.zeros((kv_dev, length, HD), jnp.float32)
    key_total, query_parts = lax.scan(
        one_head, key_start, (queries, teacher_q, teacher_k, jnp.arange(heads_dev, dtype=jnp.int32))
    )
    key_rows = lax.psum_scatter(
        key_total.astype(jnp.bfloat16), "sec", scatter_dimension=1, tiled=True
    ).astype(jnp.float32)
    grad_keys = (
        rotate_back(key_rows, own_cos, own_sin)
        .astype(jnp.bfloat16)
        .transpose(1, 0, 2)
        .reshape(rows, kv_dev * HD)
    )
    grad_queries = query_parts.transpose(1, 0, 2).reshape(rows, heads_dev * HD)
    contract = (((1,), (1,)), ((), ()))
    term = lax.dot_general(grad_queries, w_query, contract, preferred_element_type=jnp.float32)
    grad_rows = lax.psum_scatter(
        (
            term + lax.dot_general(grad_keys, w_key, contract, preferred_element_type=jnp.float32)
        ).astype(jnp.bfloat16),
        "head",
        scatter_dimension=0,
        tiled=True,
    )
    contract = (((0,), (0,)), ((), ()))
    part_q = lax.dot_general(tokens, grad_queries, contract, preferred_element_type=jnp.float32)
    part_k = lax.dot_general(tokens, grad_keys, contract, preferred_element_type=jnp.float32)
    weight_rows = lax.psum_scatter(
        jnp.concatenate([part_q, part_k], axis=1).astype(jnp.bfloat16),
        ("sec", "seq"),
        scatter_dimension=0,
        tiled=True,
    ).astype(jnp.float32)
    grad_query = weight_rows[:, : heads_dev * HD].astype(jnp.bfloat16)
    grad_key = weight_rows[:, heads_dev * HD :].astype(jnp.bfloat16)
    return (grad_rows[None], grad_query, grad_key)


def solution(mesh):
    return jax.shard_map(
        shards,
        mesh=mesh,
        in_specs=(
            P("seq", "sec", None),
            P(None, "head"),
            P(None, "head"),
            P("seq", "head", "sec"),
            P("seq", "head", "sec"),
            P(),
            P(),
        ),
        out_specs=(
            P("seq", ("sec", "head"), None),
            P(("sec", "seq"), "head"),
            P(("sec", "seq"), "head"),
        ),
        check_vma=False,
    )
```

profile of v0, /device:TPU:0, one launch (start us, length us, event | category | flops | bytes accessed | tf_op | source)
XLA Modules:
  0.0 529.0 jit_solution(6241857528726214113)
XLA Ops:
  8.2 6.4 %copy.25 = bf16[1,256,8192]{1,2,0:T(8,128)(2,1)} copy(bf16[1,256,8192]{2,1,0:T(8,128)(2,1)} %param.14) | data formatting | bytes 8388608 | tf_op args[3]
  14.6 6.4 %copy.26 = bf16[256,64,128]{2,0,1:T(8,128)(2,1)} copy(bf16[256,64,128]{0,2,1:T(8,128)(2,1)} %bitcast.176) | data formatting | bytes 8388608 | tf_op jit(solution)/shard_map/reshape;squeeze | solution.py:87
  20.9 6.4 %copy.27 = bf16[1,256,8192]{1,2,0:T(8,128)(2,1)} copy(bf16[1,256,8192]{2,1,0:T(8,128)(2,1)} %param.15) | data formatting | bytes 8388608 | tf_op args[4]
  27.3 6.4 %copy.28 = bf16[256,64,128]{2,0,1:T(8,128)(2,1)} copy(bf16[256,64,128]{0,2,1:T(8,128)(2,1)} %bitcast.177) | data formatting | bytes 8388608 | tf_op jit(solution)/shard_map/reshape;squeeze | solution.py:88
  33.7 4.4 gather_fusion.2
  38.1 4.3 gather_fusion.3
  48.9 8.1 %all-to-all-start = ((bf16[16,4,256,128]{3,2,1,0:T(8,128)(2,1)}), bf16[16,4,256,128]{3,2,1,0:T(8,128)(2,1)}, u32[]{:S(2)}, u32[]{:S(2)}) async-start(bf16[16,4,256,128]{3,2,1,0:T(8,128)(2,1)} %broadcast_select_fusion), calls=%async_computation | async-start | bytes 8388608 | tf_op jit(solution)/shard_map/all_to_all | solution.py:107
  57.2 6.4 %copy.34 = bf16[512,4096]{1,0:T(8,128)(2,1)} copy(bf16[512,4096]{0,1:T(8,128)(2,1)} %bitcast.180) | data formatting | bytes 8388608 | tf_op jit(solution)/shard_map/dot_general | solution.py:74
  63.6 60.9 %all-to-all-done = bf16[16,4,256,128]{3,2,1,0:T(8,128)(2,1)} async-done(((bf16[16,4,256,128]{3,2,1,0:T(8,128)(2,1)}), bf16[16,4,256,128]{3,2,1,0:T(8,128)(2,1)}, u32[]{:S(2)}, u32[]{:S(2)}) %all-to-all-start) | async-done | bytes 4194336 | tf_op jit(solution)/shard_map/all_to_all | solution.py:107
  127.5 8.7 %all-to-all-start.1 = ((bf16[16,4,256,128]{3,2,1,0:T(8,128)(2,1)}), bf16[16,4,256,128]{3,2,1,0:T(8,128)(2,1)}, u32[]{:S(2)}, u32[]{:S(2)}) async-start(bf16[16,4,256,128]{3,2,1,0:T(8,128)(2,1)} %bitcast.174), calls=%async_computation.1 | async-start | bytes 8388608 | tf_op jit(solution)/shard_map/all_to_all | solution.py:108
  136.4 6.3 %fusion.50 = f32[1,1024,128]{1,2,0:T(8,128)S(1)} fusion(bf16[4096,128]{1,0:T(8,128)(2,1)S(1)} %copy-done, bf16[1,1024,4096]{2,1,0:T(8,128)(2,1)} %param.11), kind=kOutput, calls=%fused_computation.58 | convolution fusion | flops 1073741824 | bytes 9961472 | tf_op jit(solution)/shard_map/dot_general | solution.py:80
  143.8 56.9 %all_gather.3 = bf16[1,2048,128]{1,2,0:T(8,128)(2,1)S(1)} all-gather(bf16[1,1024,128]{1,2,0:T(8,128)(2,1)S(1)} %pad_maximum_fusion.2), channel_id=1, replica_groups=mesh['sec'=2,'head'=8,'seq'=8] {'sec'}, dimensions={1}, use_global_device_ids=true | all-gather | bytes 786432 | tf_op jit(solution)/shard_map/all_gather | solution.py:85
  201.0 8.2 %fusion.47 = f32[4,1024,128]{1,2,0:T(8,128)S(1)} fusion(bf16[4,128,4096]{2,1,0:T(8,128)(2,1)} %bitcast.181, bf16[1,1024,4096]{2,1,0:T(8,128)(2,1)} %param.11), kind=kOutput, calls=%fused_computation.57 | convolution fusion | flops 4294967296 | bytes 14680064 | tf_op jit(solution)/shard_map/dot_general | solution.py:74
  210.6 4.3 gather_fusion
  217.3 4.3 gather_fusion.1
  221.7 84.4 %while.14 = (s32[]{:T(128)}, f32[1,2048,128]{2,1,0:T(8,128)S(1)}, bf16[4,1024,128]{1,2,0:T(8,128)(2,1)}, bf16[4,1024,128]{1,2,0:T(8,128)(2,1)}, bf16[1,2048,128]...) while((s32[]{:T(128)}, f32[1,2048,128]{2,1,0:T(8,128)S(1)}, ...), condition=%wide.region_5.7_spmd.clone, body=%wide.region_0.6_spmd.clone.sunk | while | flops 2216292352 | bytes 82392728 | solution.py:146
  227.7 5.6 %fusion.100 = (f32[1024]{0:T(1024)S(1)}, f32[1024]{0:T(1024)S(1)}) fusion(f32[1024,2048]{1,0:T(8,128)S(1)} %get-tuple-element.268, s32[2048]{0:T(1024)S(1)} %get-tuple-element.309, f32[1024]{0:T(1024)S(1)} %get-tuple-element.269, s32[1024]{0:T(1024)S(1)} %get-tuple-element.308, f32[1024]{0:T(1024)S(1)} %get-tuple-element.270, f32[1024,2048]{1,0:T(8,128)S(1)} %fusion.98), kind=kLoop, calls=%fused_computation.12.clone.1 | loop fusion | flops 23066624 | bytes 16805888 | tf_op jit(solution)/shard_map/while/body/eval_jaxpr/reduce_sum | solution.py:50
  233.3 5.8 %multiply_convert_fusion.2 = bf16[1024,2048]{1,0:T(8,128)(2,1)S(1)} fusion(f32[1024,2048]{1,0:T(8,128)S(1)} %get-tuple-element.268, f32[1024,2048]{1,0:T(8,128)S(1)} %fusion.98, s32[2048]{0:T(1024)S(1)} %get-tuple-element.309, f32[1024]{0:T(1024)S(1)} %get-tuple-element.271, f32[1024]{0:T(1024)S(1)} %get-tuple-element.270, ...), kind=kLoop, calls=%fused_computation.9.clone.1 | loop fusion | flops 29360128 | bytes 21000192 | tf_op jit(solution)/shard_map/while/body/eval_jaxpr/convert_element_type | solution.py:132
  245.4 3.3 fusion.99
  248.7 5.6 %fusion.100 = (f32[1024]{0:T(1024)S(1)}, f32[1024]{0:T(1024)S(1)}) fusion(f32[1024,2048]{1,0:T(8,128)S(1)} %get-tuple-element.268, s32[2048]{0:T(1024)S(1)} %get-tuple-element.309, f32[1024]{0:T(1024)S(1)} %get-tuple-element.269, s32[1024]{0:T(1024)S(1)} %get-tuple-element.308, f32[1024]{0:T(1024)S(1)} %get-tuple-element.270, f32[1024,2048]{1,0:T(8,128)S(1)} %fusion.98), kind=kLoop, calls=%fused_computation.12.clone.1 | loop fusion | flops 23066624 | bytes 16805888 | tf_op jit(solution)/shard_map/while/body/eval_jaxpr/reduce_sum | solution.py:50
  254.3 5.8 %multiply_convert_fusion.2 = bf16[1024,2048]{1,0:T(8,128)(2,1)S(1)} fusion(f32[1024,2048]{1,0:T(8,128)S(1)} %get-tuple-element.268, f32[1024,2048]{1,0:T(8,128)S(1)} %fusion.98, s32[2048]{0:T(1024)S(1)} %get-tuple-element.309, f32[1024]{0:T(1024)S(1)} %get-tuple-element.271, f32[1024]{0:T(1024)S(1)} %get-tuple-element.270, ...), kind=kLoop, calls=%fused_computation.9.clone.1 | loop fusion | flops 29360128 | bytes 21000192 | tf_op jit(solution)/shard_map/while/body/eval_jaxpr/convert_element_type | solution.py:132
  269.8 5.6 %fusion.100 = (f32[1024]{0:T(1024)S(1)}, f32[1024]{0:T(1024)S(1)}) fusion(f32[1024,2048]{1,0:T(8,128)S(1)} %get-tuple-element.268, s32[2048]{0:T(1024)S(1)} %get-tuple-element.309, f32[1024]{0:T(1024)S(1)} %get-tuple-element.269, s32[1024]{0:T(1024)S(1)} %get-tuple-element.308, f32[1024]{0:T(1024)S(1)} %get-tuple-element.270, f32[1024,2048]{1,0:T(8,128)S(1)} %fusion.98), kind=kLoop, calls=%fused_computation.12.clone.1 | loop fusion | flops 23066624 | bytes 16805888 | tf_op jit(solution)/shard_map/while/body/eval_jaxpr/reduce_sum | solution.py:50
  275.4 5.8 %multiply_convert_fusion.2 = bf16[1024,2048]{1,0:T(8,128)(2,1)S(1)} fusion(f32[1024,2048]{1,0:T(8,128)S(1)} %get-tuple-element.268, f32[1024,2048]{1,0:T(8,128)S(1)} %fusion.98, s32[2048]{0:T(1024)S(1)} %get-tuple-element.309, f32[1024]{0:T(1024)S(1)} %get-tuple-element.271, f32[1024]{0:T(1024)S(1)} %get-tuple-element.270, ...), kind=kLoop, calls=%fused_computation.9.clone.1 | loop fusion | flops 29360128 | bytes 21000192 | tf_op jit(solution)/shard_map/while/body/eval_jaxpr/convert_element_type | solution.py:132
  290.8 5.6 %fusion.100 = (f32[1024]{0:T(1024)S(1)}, f32[1024]{0:T(1024)S(1)}) fusion(f32[1024,2048]{1,0:T(8,128)S(1)} %get-tuple-element.268, s32[2048]{0:T(1024)S(1)} %get-tuple-element.309, f32[1024]{0:T(1024)S(1)} %get-tuple-element.269, s32[1024]{0:T(1024)S(1)} %get-tuple-element.308, f32[1024]{0:T(1024)S(1)} %get-tuple-element.270, f32[1024,2048]{1,0:T(8,128)S(1)} %fusion.98), kind=kLoop, calls=%fused_computation.12.clone.1 | loop fusion | flops 23066624 | bytes 16805888 | tf_op jit(solution)/shard_map/while/body/eval_jaxpr/reduce_sum | solution.py:50
  296.4 5.8 %multiply_convert_fusion.2 = bf16[1024,2048]{1,0:T(8,128)(2,1)S(1)} fusion(f32[1024,2048]{1,0:T(8,128)S(1)} %get-tuple-element.268, f32[1024,2048]{1,0:T(8,128)S(1)} %fusion.98, s32[2048]{0:T(1024)S(1)} %get-tuple-element.309, f32[1024]{0:T(1024)S(1)} %get-tuple-element.271, f32[1024]{0:T(1024)S(1)} %get-tuple-element.270, ...), kind=kLoop, calls=%fused_computation.9.clone.1 | loop fusion | flops 29360128 | bytes 21000192 | tf_op jit(solution)/shard_map/while/body/eval_jaxpr/convert_element_type | solution.py:132
  307.3 10.2 %fusion.36 = bf16[4096,512]{0,1:T(8,128)(2,1)} fusion(bf16[1024,512]{0,1:T(8,128)(2,1)} %bitcast.182, bf16[1,1024,4096]{2,1,0:T(8,128)(2,1)} %param.11), kind=kOutput, calls=%fused_computation.48 | convolution fusion | flops 4297064448 | bytes 13631488 | tf_op jit(solution)/shard_map/dot_general | solution.py:170
  317.5 7.8 %reduce-scatter.4.cloned.1.call-done = bf16[1,1024,128]{1,2,0:T(8,128)(2,1)} async-done(((bf16[1,2048,128]{1,2,0:T(8,128)(2,1)}), bf16[1,1024,128]{1,2,0:T(8,128)(2,1)}) %reduce-scatter.4.cloned.1.call-update) | async-done | bytes 262160 | tf_op jit(solution)/shard_map/reduce_scatter | solution.py:149
  326.4 4.8 fusion.42
  334.3 10.6 %fusion.72 = f32[1024,4096]{1,0:T(8,128)} fusion(bf16[1024,512]{0,1:T(8,128)(2,1)S(1)} %bitcast.183, bf16[4096,512]{1,0:T(8,128)(2,1)} %param.12), kind=kOutput, calls=%fused_computation.112 | convolution fusion | flops 4294967296 | bytes 22020096 | tf_op jit(solution)/shard_map/dot_general | solution.py:160
  344.9 11.4 %add_convert_fusion.1 = bf16[1024,4096]{1,0:T(8,128)(2,1)} fusion(f32[1024,4096]{1,0:T(8,128)} %fusion.72, bf16[4096,128]{1,0:T(8,128)(2,1)S(1)} %copy-done, bf16[1024,64]{0,1:T(8,128)(2,1)S(1)} %get-tuple-element.188, bf16[1024,64]{0,1:T(8,128)(2,1)S(1)} %get-tuple-element.187), kind=kOutput, calls=%fused_computation.38 | convolution fusion | flops 1082654720 | bytes 26476544 | tf_op jit(solution)/shard_map/dot_general | solution.py:163
  356.3 47.7 %reduce-scatter.8.cloned.1.call-done = bf16[256,640]{0,1:T(8,128)(2,1)} async-done(((bf16[4096,640]{0,1:T(8,128)(2,1)}), bf16[256,640]{0,1:T(8,128)(2,1)}) %reduce-scatter.8.cloned.1.call-update) | async-done | bytes 327696 | tf_op jit(solution)/shard_map/reduce_scatter | solution.py:172
  407.5 115.0 %reduce-scatter.6.cloned.1.call-done = bf16[128,4096]{1,0:T(8,128)(2,1)} async-done(((bf16[1024,4096]{1,0:T(8,128)(2,1)}), bf16[128,4096]{1,0:T(8,128)(2,1)}) %reduce-scatter.6.cloned.1.call-update) | async-done | bytes 1048592 | tf_op jit(solution)/shard_map/reduce_scatter | solution.py:161
  (81 shorter events, 59.6 us)
Async XLA Ops:
  7.2 129.2 %copy-start = (bf16[4096,128]{1,0:T(8,128)(2,1)S(1)}, bf16[4096,128]{1,0:T(8,128)(2,1)}, u32[]{:S(2)}) copy-start(bf16[4096,128]{1,0:T(8,128)(2,1)} %param.13) | copy-start | bytes 3145732
  46.6 10.4 %copy-start.3 = (s32[32]{0:T(128)S(1)}, s32[32]{0:T(128)}, u32[]{:S(2)}) copy-start(s32[32]{0:T(128)} %param.16) | copy-start | bytes 388
  48.9 14.6 %copy-start.5 = (s32[16]{0:T(128)S(1)}, s32[16]{0:T(128)}, u32[]{:S(2)}) copy-start(s32[16]{0:T(128)} %param.17) | copy-start | bytes 196
  48.9 75.6 %all-to-all-start = ((bf16[16,4,256,128]{3,2,1,0:T(8,128)(2,1)}), bf16[16,4,256,128]{3,2,1,0:T(8,128)(2,1)}, u32[]{:S(2)}, u32[]{:S(2)}) async-start(bf16[16,4,256,128]{3,2,1,0:T(8,128)(2,1)} %broadcast_select_fusion), calls=%async_computation | async-start | bytes 8388608 | tf_op jit(solution)/shard_map/all_to_all | solution.py:107
  127.5 89.7 %all-to-all-start.1 = ((bf16[16,4,256,128]{3,2,1,0:T(8,128)(2,1)}), bf16[16,4,256,128]{3,2,1,0:T(8,128)(2,1)}, u32[]{:S(2)}, u32[]{:S(2)}) async-start(bf16[16,4,256,128]{3,2,1,0:T(8,128)(2,1)} %bitcast.174), calls=%async_computation.1 | async-start | bytes 8388608 | tf_op jit(solution)/shard_map/all_to_all | solution.py:108
  136.2 189.1 %reduce-scatter.4.cloned.1.call-start = ((), (), s32[]{:S(2)}) async-start(), calls=%async_computation.5 | async-start | bytes 786432 | tf_op jit(solution)/shard_map/reduce_scatter | solution.py:149
  221.8 2.5 copy-start.1
  242.9 2.5 copy-start.1
  263.9 2.5 copy-start.1
  285.0 2.5 copy-start.1
  307.1 97.0 %reduce-scatter.8.cloned.1.call-start = ((), (), s32[]{:S(2)}) async-start(), calls=%async_computation.7 | async-start | bytes 5570560 | tf_op jit(solution)/shard_map/reduce_scatter | solution.py:172
  326.3 4.9 copy-start.2
  331.2 3.1 copy-start.4
  334.2 188.2 %reduce-scatter.6.cloned.1.call-start = ((), (), s32[]{:S(2)}) async-start(), calls=%async_computation.6 | async-start | bytes 9437184 | tf_op jit(solution)/shard_map/reduce_scatter | solution.py:161
Sparse Core Ops, SparseCore 0:
  307.2 18.0 reduce-scatter.3
  334.4 69.6 reduce-scatter.7
  408.9 113.4 reduce-scatter.5
where the time goes:
time: 531 us; the launch traced here: 529 us
  waiting for transfers between devices  231 us (44%)
  matrix products  86.4 us (16%)
  other arithmetic  61.5 us (12%)
  local copies, waits for them, and re-layouts  61 us (11%)
  blocking collectives  56.9 us (11%)
  starting transfers between devices  17.2 us (3%)
  between operations  14 us (3%)
    reduce_scatter x1, waiting for transfers between devices, shards(): lax.psum_scatter((term + lax.dot_general(grad_keys, w_key, contract, pref...  115 us
    all_to_all x1, waiting for transfers between devices, shards(): lax.all_to_all(sent_q, ('sec', 'head'), split_axis=0, concat_axis=0, tile...  60.9 us
    all_gather x1, blocking collectives, shards(): all_keys = lax.all_gather(own_keys, 'sec', axis=1, tiled=True)  56.9 us
    reduce_scatter x1, waiting for transfers between devices, shards(): lax.psum_scatter(jnp.concatenate([part_q, part_k], axis=1).astype(jnp.bfl...  47.7 us
    convert_element_type x4, other arithmetic, one_head(): score_grads = ((p_student - p_teacher) * grad_scale).astype(jnp.bfloat16)  23.2 us
    reduce_sum x4, other arithmetic, masked_softmax(): return weights / jnp.sum(weights, axis=-1, keepdims=True)  22.4 us
    unnamed x15, local copies, waits for them, and re-layouts  14.7 us
    dot_general x4, matrix products, one_head(): lax.dot_general(query, key_one, contract, preferred_element_type=jnp.floa...  13.3 us
  transfers between devices with their start and end apart: 5, of which 4 were waited for; matrix products, arithmetic and copies ran while one was open for 13% of the time, Pallas kernels for 0%

commit v1 on v0

v1 whole, which is shorter than its diff:
```python
import math

import jax
import jax.numpy as jnp
from jax import lax
from jax.experimental import pallas as pl
from jax.experimental.pallas import tpu as pltpu
from jax.sharding import PartitionSpec as P

HD = 128
QB = 128
NBLK = 16
HALF_BLKS = 8
HEADS = 4
TH_SEC = 64
GROUPS = 8
ROWS = 1024
LEN = 2048
TROWS = 256
D = 4096
GW = 640
QW = 512
CK = 256
MIB = 1024 * 1024

rope_base = 500000.0
grad_scale = 16.0
scale = 1.0 / math.sqrt(HD)
MESH = pl.DeviceIdType.MESH
ANY = pl.BlockSpec(memory_space=pl.ANY)
VMEM = pl.BlockSpec(memory_space=pltpu.VMEM)
SMEM = pl.BlockSpec(memory_space=pltpu.SMEM)
DMA = pltpu.SemaphoreType.DMA
F32 = jnp.float32
BF16 = jnp.bfloat16


def rope_rows(block_order, sec):
    own = lax.dynamic_slice_in_dim(block_order, sec * HALF_BLKS, HALF_BLKS, 0)
    positions = (own[:, None] * QB + jnp.arange(QB, dtype=jnp.int32)[None, :]).reshape(-1)
    half = HD // 2
    freqs = rope_base ** (-(jnp.arange(half, dtype=F32) * 2.0) / HD)
    angles = positions.astype(F32)[:, None] * freqs[None, :]
    cosine, sine = jnp.cos(angles), jnp.sin(angles)
    return jnp.stack(
        [
            jnp.concatenate([cosine, cosine], axis=1),
            jnp.concatenate([-sine, sine], axis=1),
        ]
    )


def section_slots(match_ref, group, section):
    low, high = jnp.int32(TH_SEC - 1), jnp.int32(0)
    for i in range(HEADS):
        local = match_ref[group * HEADS + i] - section * TH_SEC
        inside = (local >= 0) & (local < TH_SEC)
        low = jnp.minimum(low, jnp.where(inside, local, TH_SEC - 1))
        high = jnp.maximum(high, jnp.where(inside, local, 0))
    return low, high


def pick_kernel(match_ref, tk_ref, tq_ref, k_out, q_out, k_v, q_v, in_sems, out_sems):
    sec = lax.axis_index("sec")
    copies = []
    for g in range(GROUPS):
        for j, local in enumerate(section_slots(match_ref, g, sec)):
            columns = pl.ds(pl.multiple_of(local * HD, HD), HD)
            for a, (src, held, dst) in enumerate(((tk_ref, k_v, k_out), (tq_ref, q_v, q_out))):
                place = held.at[g // 2, g % 2, j]
                load = pltpu.make_async_copy(src.at[0, :, columns], place, in_sems.at[a, g * 2 + j])
                load.start()
                store = pltpu.make_async_copy(
                    place, dst.at[g // 2, g % 2, j], out_sems.at[a, g * 2 + j]
                )
                copies.append((load, store))
    for load, store in copies:
        load.wait()
        store.start()
    for load, store in copies:
        store.wait()


def pick(match, teacher_keys, teacher_queries):
    shape = (4, 2, 2, TROWS, HD)
    return pl.pallas_call(
        pick_kernel,
        out_shape=(jax.ShapeDtypeStruct(shape, BF16), jax.ShapeDtypeStruct(shape, BF16)),
        in_specs=[SMEM, ANY, ANY],
        out_specs=(ANY, ANY),
        scratch_shapes=[
            pltpu.VMEM(shape, BF16),
            pltpu.VMEM(shape, BF16),
            DMA((2, 16)),
            DMA((2, 16)),
        ],
        name="pick",
    )(match, teacher_keys, teacher_queries)


def spread_kernel(
    sk, sq, tok, wq, wk, rope,
    q_out, keys_out, gotk, gotq, w2,
    rope_v, tok_v, w_v, k_v, zk, zq,
    load_sem, own_sem, zs, zr, pks, pkr, cks, ckr, rks, rkr, qps, qpr, qxs, qxr,
    keys_s, keys_r, w1s, w1r, wys, wyr, wrs, wrr, wcs, wcr,
):
    sec, head, seq = lax.axis_index("sec"), lax.axis_index("head"), lax.axis_index("seq")
    z, xh = head // 2, head % 2
    y, c = seq // 2, seq % 2
    partner = {"sec": 1 - sec}
    cross = {"sec": 1 - sec, "head": z * 2 + 1 - xh}
    far = {"head": z * 2 + 1 - xh}
    core = {"seq": y * 2 + 1 - c}
    up = {"seq": ((y + 1) % 4) * 2 + c}
    down = {"seq": ((y + 3) % 4) * 2 + c}

    def depth(d):
        return {"head": ((z + d) % 4) * 2 + xh}

    def send(src, dst, ss, rs, where):
        return pltpu.make_async_remote_copy(
            src_ref=src, dst_ref=dst, send_sem=ss, recv_sem=rs, device_id=where, device_id_type=MESH
        )

    loads = [
        pltpu.make_async_copy(wq, w_v.at[:, pl.ds(0, QW)], load_sem.at[4]),
        pltpu.make_async_copy(wk, w_v.at[:, pl.ds(QW, HD)], load_sem.at[5]),
        pltpu.make_async_copy(rope, rope_v, load_sem.at[6]),
    ]
    for load in loads:
        load.start()

    def token_load(r):
        rows = pl.ds(pl.multiple_of(r * 256, 256), 256)
        return pltpu.make_async_copy(tok.at[0, rows], tok_v.at[rows], load_sem.at[r])

    for r in range(4):
        token_load(r).start()

    barrier = pltpu.get_barrier_semaphore()
    greet = [partner, cross, far, core, up, down, depth(1), depth(2), depth(3)]
    for where in greet:
        pl.semaphore_signal(barrier, inc=1, device_id=where, device_id_type=MESH)
    pl.semaphore_wait(barrier, len(greet))

    zcopies = []
    for d in (1, 3, 2):
        to = (z + d) % 4
        for a, (src, dst) in enumerate(((sk, zk), (sq, zq))):
            copy = send(src.at[to], dst.at[d - 1], zs.at[a, d - 1], zr.at[a, d - 1], depth(d))
            copy.start()
            zcopies.append(copy)

    def krows(d, xhs):
        return pl.ds(pl.multiple_of((((z + 4 - d) % 4) * 2 + xhs) * TROWS, TROWS), TROWS)

    def qrows(d, xhs):
        return pl.ds(
            pl.multiple_of(((((z + 4 - d) % 4) * 2 + xhs) % 4) * TROWS, TROWS), TROWS
        )

    def held(d):
        return (sk.at[z], sq.at[z]) if d == 0 else (zk.at[d - 1], zq.at[d - 1])

    def along_x(d):
        kd, qd = held(d)
        half = ((z + 4 - d) % 4) // 2
        mine = gotk.at[sec, :, krows(d, xh)]
        mine_q = gotq.at[sec, :, qrows(d, xh)]
        return dict(
            ck=send(kd.at[1 - xh], mine, cks.at[d], ckr.at[d], cross),
            pk=send(kd.at[xh], mine, pks.at[d], pkr.at[d], partner),
            qx=send(
                qd.at[1 - xh], mine_q, qxs.at[d], qxr.at[d, sec],
                {"sec": half, "head": z * 2 + 1 - xh},
            ),
            qp=send(qd.at[xh], mine_q, qps.at[d], qpr.at[d], partner),
            lk=pltpu.make_async_copy(kd.at[xh], mine, own_sem.at[0, d]),
            lq=pltpu.make_async_copy(qd.at[xh], mine_q, own_sem.at[1, d]),
            half=half,
        )

    def start_x(d):
        m = along_x(d)
        m["ck"].start()
        m["pk"].start()
        m["qx"].start()

        @pl.when(m["half"] != sec)
        def _():
            m["qp"].start()

        m["lk"].start()

        @pl.when(m["half"] == sec)
        def _():
            m["lq"].start()

    def relay(d):
        got = gotk.at[1 - sec, :, krows(d, 1 - xh)]
        return send(got, got, rks.at[d], rkr.at[d], partner)

    start_x(0)

    for load in loads:
        load.wait()

    def piece(ref, yy, cc, j):
        start = ((yy % 4) * 2 + cc) * 512 + j * 256
        return ref.at[pl.ds(pl.multiple_of(start, 256), 256)]

    first = []
    for j in range(2):
        copy = send(piece(w_v, y, c, j), piece(w2, y, c, j), w1s.at[j], w1r.at[j], cross)
        copy.start()
        first.append(copy)

    def project(r, _):
        token_load(r).wait()
        rows = pl.ds(pl.multiple_of(r * 256, 256), 256)
        product = jnp.dot(tok_v[rows, :], w_v[...], preferred_element_type=F32)
        cosine, sine = rope_v[0, rows, :], rope_v[1, rows, :]
        for h in range(HEADS + 1):
            part = product[:, h * HD : (h + 1) * HD]
            part = (part * cosine + pltpu.roll(part, HD // 2, axis=1) * sine).astype(BF16)
            if h < HEADS:
                q_out[rows, h * HD : (h + 1) * HD] = part
            else:
                k_v[rows, :] = part
        return 0

    lax.fori_loop(0, 4, project, 0)
    key_rows = keys_out.at[pl.ds(pl.multiple_of(sec * ROWS, ROWS), ROWS)]
    key_send = send(k_v, key_rows, keys_s, keys_r, partner)
    key_send.start()
    key_own = pltpu.make_async_copy(k_v, key_rows, own_sem.at[2, 0])
    key_own.start()

    relays = []

    def wait_relay(d):
        got = gotk.at[1 - sec, :, krows(d, 1 - xh)]
        send(got, got, cks.at[d], ckr.at[d], cross).wait_recv()
        copy = relay(d)
        copy.start()
        relays.append(copy)

    wait_relay(0)
    for d in (1, 3):
        zcopies[0 if d == 1 else 2].wait_recv()
        zcopies[1 if d == 1 else 3].wait_recv()
        start_x(d)

    wcopies = []

    def forward(src_y, j, sems, rsems, index, where):
        ref = piece(w2, src_y, c, j)
        copy = send(ref, ref, sems.at[index], rsems.at[index], where)
        copy.start()
        wcopies.append(copy)

    def wait_piece(src_y, cc, j, sem, rsem):
        ref = piece(w2, src_y, cc, j)
        send(ref, ref, sem, rsem, core).wait_recv()

    for j in range(2):
        wait_piece(y, c, j, w1s.at[j], w1r.at[j])
        forward(y, j, wys, wyr, j, up)
        forward(y, j, wys, wyr, 2 + j, down)
        forward(y, j, wcs, wcr, j, core)
    wait_relay(1)
    wait_relay(3)
    zcopies[4].wait_recv()
    zcopies[5].wait_recv()
    start_x(2)
    wait_piece(y + 3, c, 0, wys.at[0], wyr.at[0])
    forward(y + 3, 0, wrs, wrr, 0, up)
    forward(y + 3, 0, wcs, wcr, 2, core)
    wait_piece(y + 1, c, 1, wys.at[3], wyr.at[3])
    forward(y + 1, 1, wrs, wrr, 1, down)
    forward(y + 1, 1, wcs, wcr, 3, core)
    wait_relay(2)
    wait_piece(y + 3, c, 1, wys.at[1], wyr.at[1])
    forward(y + 3, 1, wcs, wcr, 4, core)
    wait_piece(y + 1, c, 0, wys.at[2], wyr.at[2])
    forward(y + 1, 0, wcs, wcr, 5, core)
    wait_piece(y + 2, c, 0, wrs.at[0], wrr.at[0])
    forward(y + 2, 0, wcs, wcr, 6, core)
    wait_piece(y + 2, c, 1, wrs.at[1], wrr.at[1])
    forward(y + 2, 1, wcs, wcr, 7, core)

    for index, (dy, j) in enumerate(((0, 0), (0, 1), (3, 0), (1, 1), (3, 1), (1, 0), (2, 0), (2, 1))):
        wait_piece(y + dy, 1 - c, j, wcs.at[index], wcr.at[index])
    other_rows = keys_out.at[pl.ds(pl.multiple_of((1 - sec) * ROWS, ROWS), ROWS)]
    send(k_v, other_rows, keys_s, keys_r, partner).wait_recv()
    for d in range(4):
        m = along_x(d)
        got = gotk.at[1 - sec, :, krows(d, xh)]
        send(got, got, pks.at[d], pkr.at[d], partner).wait_recv()
        got = gotk.at[sec, :, krows(d, 1 - xh)]
        send(got, got, rks.at[d], rkr.at[d], partner).wait_recv()

        @pl.when(m["half"] == sec)
        def _():
            got = gotq.at[1 - sec, :, qrows(d, xh)]
            send(got, got, qps.at[d], qpr.at[d], partner).wait_recv()
            for source in range(2):
                got = gotq.at[source, :, qrows(d, 1 - xh)]
                send(got, got, qxs.at[d], qxr.at[d, source], cross).wait_recv()
            m["lq"].wait()

        @pl.when(m["half"] != sec)
        def _():
            m["qp"].wait_send()

        m["lk"].wait()
        m["ck"].wait_send()
        m["pk"].wait_send()
        m["qx"].wait_send()
    key_own.wait()
    key_send.wait_send()
    for copy in zcopies + first + relays + wcopies:
        copy.wait_send()


def spread(picked_k, picked_q, inputs, w_query, w_key, rope):
    return pl.pallas_call(
        spread_kernel,
        out_shape=(
            jax.ShapeDtypeStruct((ROWS, QW), BF16),
            jax.ShapeDtypeStruct((LEN, HD), BF16),
            jax.ShapeDtypeStruct((2, 2, LEN, HD), BF16),
            jax.ShapeDtypeStruct((2, 2, ROWS, HD), BF16),
            jax.ShapeDtypeStruct((D, GW), BF16),
        ),
        in_specs=[ANY] * 6,
        out_specs=(VMEM, ANY, ANY, ANY, ANY),
        scratch_shapes=[
            pltpu.VMEM((2, ROWS, HD), F32),
            pltpu.VMEM((ROWS, D), BF16),
            pltpu.VMEM((D, GW), BF16),
            pltpu.VMEM((ROWS, HD), BF16),
            pltpu.VMEM((3, 2, 2, TROWS, HD), BF16),
            pltpu.VMEM((3, 2, 2, TROWS, HD), BF16),
            DMA((7,)),
            DMA((3, 4)),
            DMA((2, 3)), DMA((2, 3)),
            DMA((4,)), DMA((4,)),
            DMA((4,)), DMA((4,)),
            DMA((4,)), DMA((4,)),
            DMA((4,)), DMA((4,)),
            DMA((4,)), DMA((4, 2)),
            DMA, DMA,
            DMA((2,)), DMA((2,)),
            DMA((4,)), DMA((4,)),
            DMA((2,)), DMA((2,)),
            DMA((8,)), DMA((8,)),
        ],
        compiler_params=pltpu.CompilerParams(
            collective_id=1, has_side_effects=True, vmem_limit_bytes=48 * MIB
        ),
        name="spread",
    )(picked_k, picked_q, inputs, w_query, w_key, rope)


def attend_kernel(
    order_ref, match_ref, q_ref, keys, gotq, gotk, rope,
    qg_ref, own_ref, other_ref,
    kp, tkp, tqv, st, g_acc, dk, sems, qsems,
):
    sec, head = lax.axis_index("sec"), lax.axis_index("head")
    exponent = scale * math.log2(math.e)
    lows = [section_slots(match_ref, head, section)[0] for section in range(2)]
    places = []
    for i in range(HEADS):
        entry = match_ref[head * HEADS + i]
        section = entry // TH_SEC
        low = jnp.where(section == 0, lows[0], lows[1])
        slot = jnp.where(entry - section * TH_SEC == low, 0, 1)
        places.append((section, slot))
    copies = []
    for i, (section, slot) in enumerate(places):
        copies.append(pltpu.make_async_copy(gotq.at[section, slot], tqv.at[i], qsems.at[i]))
        copies[-1].start()
    for b in range(NBLK):
        to = pl.ds(pl.multiple_of(order_ref[b] * QB, QB), QB)
        at = pl.ds(b * QB, QB)
        copies.append(pltpu.make_async_copy(keys.at[at], kp.at[to], sems.at[4, b]))
        copies[-1].start()
        for i, (section, slot) in enumerate(places):
            copies.append(
                pltpu.make_async_copy(gotk.at[section, slot, at], tkp.at[i, to], sems.at[i, b])
            )
            copies[-1].start()
    dk[...] = jnp.zeros_like(dk)
    for copy in copies:
        copy.wait()

    nt = (((1,), (1,)), ((), ()))
    tn = (((0,), (0,)), ((), ()))

    def one_block(qb, _):
        rows = pl.ds(pl.multiple_of(qb * QB, QB), QB)
        block = order_ref[sec * HALF_BLKS + qb]
        last = block // 2
        queries = jnp.concatenate(
            [q_ref[rows, i * HD : (i + 1) * HD] for i in range(HEADS)], axis=0
        )

        def scores(chunk, top, masked):
            at = pl.ds(pl.multiple_of(chunk * CK, CK), CK)
            student = lax.dot_general(kp[at, :], queries, nt, preferred_element_type=F32)
            teacher = jnp.concatenate(
                [
                    lax.dot_general(tkp[i, at, :], tqv[i, rows, :], nt, preferred_element_type=F32)
                    for i in range(HEADS)
                ],
                axis=1,
            )
            both = jnp.concatenate([student, teacher], axis=1)
            if masked:
                key_at = lax.broadcasted_iota(jnp.int32, both.shape, 0) + chunk * CK
                row_at = lax.broadcasted_iota(jnp.int32, both.shape, 1) % QB + block * QB
                both = jnp.where(key_at <= row_at, both, -jnp.inf)
            st[at, :] = both
            return jnp.maximum(top, jnp.max(both.reshape(CK // 8, 8, 2 * QW), axis=0))

        top = jnp.full((8, 2 * QW), -jnp.inf, F32)
        top = lax.fori_loop(0, last, lambda chunk, t: scores(chunk, t, False), top)
        top = scores(last, top, True)
        top = jnp.max(top, axis=0, keepdims=True)

        def weights(chunk, total):
            at = pl.ds(pl.multiple_of(chunk * CK, CK), CK)
            e = jnp.exp2((st[at, :] - top) * exponent)
            st[at, :] = e
            return total + jnp.sum(e.reshape(CK // 8, 8, 2 * QW), axis=0)

        total = lax.fori_loop(0, last + 1, weights, jnp.zeros((8, 2 * QW), F32))
        inverse = grad_scale / jnp.sum(total, axis=0, keepdims=True)
        g_acc[...] = jnp.zeros_like(g_acc)

        def grads(chunk, _):
            at = pl.ds(pl.multiple_of(chunk * CK, CK), CK)
            g = (st[at, :QW] * inverse[:, :QW] - st[at, QW:] * inverse[:, QW:]).astype(BF16)
            dk[at, :] += jnp.dot(g, queries, preferred_element_type=F32)
            g_acc[...] += lax.dot_general(g, kp[at, :], tn, preferred_element_type=F32)
            return 0

        lax.fori_loop(0, last + 1, grads, 0)
        cosine, sine = rope[0, rows, :], rope[1, rows, :]
        for i in range(HEADS):
            part = g_acc[i * QB : (i + 1) * QB, :] * scale
            part = part * cosine - pltpu.roll(part, HD // 2, axis=1) * sine
            qg_ref[rows, i * HD : (i + 1) * HD] = part.astype(BF16)
        return 0

    lax.fori_loop(0, HALF_BLKS, one_block, 0)
    for b in range(HALF_BLKS):
        at = pl.ds(b * QB, QB)
        for half, ref in ((sec, own_ref), (1 - sec, other_ref)):
            block = order_ref[half * HALF_BLKS + b]
            part = dk[pl.ds(pl.multiple_of(block * QB, QB), QB), :] * scale
            ref[at, :] = part.astype(ref.dtype)


def attend(order, match, queries, keys, gotq, gotk, rope):
    return pl.pallas_call(
        attend_kernel,
        out_shape=(
            jax.ShapeDtypeStruct((ROWS, QW), BF16),
            jax.ShapeDtypeStruct((ROWS, HD), F32),
            jax.ShapeDtypeStruct((ROWS, HD), BF16),
        ),
        in_specs=[SMEM, SMEM, VMEM, ANY, ANY, ANY, VMEM],
        out_specs=(VMEM, VMEM, VMEM),
        scratch_shapes=[
            pltpu.VMEM((LEN, HD), BF16),
            pltpu.VMEM((HEADS, LEN, HD), BF16),
            pltpu.VMEM((HEADS, ROWS, HD), BF16),
            pltpu.VMEM((LEN, 2 * QW), F32),
            pltpu.VMEM((QW, HD), F32),
            pltpu.VMEM((LEN, HD), F32),
            DMA((HEADS + 1, NBLK)),
            DMA((HEADS,)),
        ],
        compiler_params=pltpu.CompilerParams(vmem_limit_bytes=48 * MIB),
        name="attend",
    )(order, match, queries, keys, gotq, gotk, rope)


def finish_kernel(
    qg, own, other, tok, wq, wk, w2, rope,
    rows_out, gq_out, gk_out,
    own_v, rope_v,
    tok_v, w_v, w2_v, gt, gk_v, key_rx, g2, k2, z_tx, z_rx, c_tx, c_rx, y_tx, y_rx, s_tx, s_rx, qg_v,
    load_sem, key_s, key_r, x_s, x_r, zs, zr, cs, cr, ys, yr, ss, sr,
):
    sec, head, seq = lax.axis_index("sec"), lax.axis_index("head"), lax.axis_index("seq")
    z, xh = head // 2, head % 2
    y, c = seq // 2, seq % 2
    partner = {"sec": 1 - sec}
    far = {"head": z * 2 + 1 - xh}
    core = {"seq": y * 2 + 1 - c}
    around_y = ({"seq": ((y + 1) % 4) * 2 + c}, {"seq": ((y + 3) % 4) * 2 + c})
    around_z = ({"head": ((z + 1) % 4) * 2 + xh}, {"head": ((z + 3) % 4) * 2 + xh})

    def send(src, dst, ss_, rs_, where):
        return pltpu.make_async_remote_copy(
            src_ref=src, dst_ref=dst, send_sem=ss_, recv_sem=rs_, device_id=where, device_id_type=MESH
        )

    loads = [
        pltpu.make_async_copy(qg, qg_v, load_sem.at[0]),
        pltpu.make_async_copy(tok.at[0], tok_v, load_sem.at[1]),
        pltpu.make_async_copy(wq, w_v.at[:, pl.ds(0, QW)], load_sem.at[2]),
        pltpu.make_async_copy(wk, w_v.at[:, pl.ds(QW, HD)], load_sem.at[3]),
        pltpu.make_async_copy(w2, w2_v, load_sem.at[4]),
    ]
    small = [
        pltpu.make_async_copy(own, own_v, load_sem.at[5]),
        pltpu.make_async_copy(rope, rope_v, load_sem.at[6]),
    ]
    for load in loads[:1] + small + loads[1:]:
        load.start()

    barrier = pltpu.get_barrier_semaphore()
    greet = [partner, far, core, *around_y, *around_z]
    for where in greet:
        pl.semaphore_signal(barrier, inc=1, device_id=where, device_id_type=MESH)
    pl.semaphore_wait(barrier, len(greet))

    key_send = send(other, key_rx, key_s, key_r, partner)
    key_send.start()
    q_send = send(qg.at[:, 1 - xh], g2, x_s.at[0], x_r.at[0], far)
    q_send.start()
    loads[0].wait()
    for b in range(HALF_BLKS):
        gt[0:QW, b * QB : (b + 1) * QB] = qg_v[b // 2, b % 2].T
    for load in small:
        load.wait()
    key_send.wait_recv()
    for b in range(HALF_BLKS):
        at = pl.ds(b * QB, QB)
        total = own_v[at, :] + key_rx[at, :].astype(F32)
        total = total * rope_v[0, at, :] - pltpu.roll(total, HD // 2, axis=1) * rope_v[1, at, :]
        total = total.astype(BF16)
        gk_v[b // 2, b % 2] = total
        gt[QW:GW, b * QB : (b + 1) * QB] = total.T
    k_send = send(gk_v.at[:, 1 - xh], k2, x_s.at[1], x_r.at[1], far)
    k_send.start()

    def weight_part(s, yy, cc):
        start = (s * 8 + (yy % 4) * 2 + cc) * 256
        return jnp.dot(
            gt[...], tok_v[:, pl.ds(pl.multiple_of(start, 256), 256)], preferred_element_type=F32
        )

    def core_copy(i):
        return send(c_tx.at[i], c_rx.at[i], cs.at[i], cr.at[i], core)

    loads[1].wait()

    def to_core(i, _):
        s, step = i % 2, i // 2
        yy = jnp.where(s == 0, y + 3 - step, y + 1 + step) % 4
        c_tx[i] = weight_part(s, yy, 1 - c).astype(BF16)
        core_copy(i).start()
        return 0

    lax.fori_loop(0, 8, to_core, 0)
    for load in loads[2:]:
        load.wait()
    q_send.wait_recv()
    k_send.wait_recv()

    nt = (((1,), (1,)), ((), ()))

    def row_term(zz, column):
        at = pl.ds(column, 1024)
        zz = zz % 4
        own = jnp.concatenate([qg_v[zz, xh], gk_v[zz, xh]], axis=1)
        theirs = jnp.concatenate([g2[zz], k2[zz]], axis=1)
        return lax.dot_general(
            own, w_v[at, :], nt, preferred_element_type=F32
        ) + lax.dot_general(theirs, w2_v[at, :], nt, preferred_element_type=F32)

    def z_copy(stream, step):
        return send(
            z_tx.at[stream, step], z_rx.at[stream, step],
            zs.at[stream, step], zr.at[stream, step], around_z[stream // 2],
        )

    def z_step(step):
        for stream in (0, 2, 1, 3):
            target = z + 3 - step if stream < 2 else z + 1 + step
            term = row_term(target, stream * 1024)
            if step > 0:
                z_copy(stream, step - 1).wait_recv()
                term = term + z_rx[stream, step - 1].astype(F32)
            if step < 3:
                z_tx[stream, step] = term.astype(BF16)
                z_copy(stream, step).start()
            else:
                rows_out[:, stream * 1024 : (stream + 1) * 1024] = term.astype(BF16)

    def y_copy(stream, step):
        return send(
            y_tx.at[stream, step], y_rx.at[stream, step],
            ys.at[stream, step], yr.at[stream, step], around_y[stream],
        )

    def y_total(stream, step):
        target = y + 3 - step if stream == 0 else y + 1 + step
        total = weight_part(stream, target, c)
        core_copy(step * 2 + stream).wait_recv()
        total = total + c_rx[step * 2 + stream].astype(F32)
        if step > 0:
            y_copy(stream, step - 1).wait_recv()
            total = total + y_rx[stream, step - 1].astype(F32)
        return total

    def y_step(step):
        for stream in range(2):
            y_tx[stream, step] = y_total(stream, step).astype(BF16)
            y_copy(stream, step).start()

    z_step(0)
    y_step(0)
    z_step(1)
    y_step(1)
    y_step(2)
    z_step(2)
    sec_copy = send(s_tx, s_rx, ss, sr, partner)
    first, second = y_total(0, 3), y_total(1, 3)
    keep = jnp.where(sec == 0, first, second)
    s_tx[...] = jnp.where(sec == 0, second, first).astype(BF16)
    sec_copy.start()
    z_step(3)
    sec_copy.wait_recv()
    keep = (keep + s_rx[...].astype(F32)).T
    gq_out[...] = keep[:, :QW].astype(BF16)
    gk_out[...] = keep[:, QW:].astype(BF16)

    for copy in (key_send, q_send, k_send, sec_copy):
        copy.wait_send()
    for i in range(8):
        core_copy(i).wait_send()
    for step in range(3):
        for stream in range(4):
            z_copy(stream, step).wait_send()
        for stream in range(2):
            y_copy(stream, step).wait_send()


def finish(qg, own, other, inputs, w_query, w_key, w2, rope):
    return pl.pallas_call(
        finish_kernel,
        out_shape=(
            jax.ShapeDtypeStruct((QB, D), BF16),
            jax.ShapeDtypeStruct((256, QW), BF16),
            jax.ShapeDtypeStruct((256, HD), BF16),
        ),
        in_specs=[ANY] * 8,
        out_specs=(VMEM, VMEM, VMEM),
        scratch_shapes=[
            pltpu.VMEM((ROWS, HD), F32),
            pltpu.VMEM((2, ROWS, HD), F32),
            pltpu.VMEM((ROWS, D), BF16),
            pltpu.VMEM((D, GW), BF16),
            pltpu.VMEM((D, GW), BF16),
            pltpu.VMEM((GW, ROWS), BF16),
            pltpu.VMEM((4, 2, QB, HD), BF16),
            pltpu.VMEM((ROWS, HD), BF16),
            pltpu.VMEM((4, QB, QW), BF16),
            pltpu.VMEM((4, QB, HD), BF16),
            pltpu.VMEM((4, 3, QB, 1024), BF16),
            pltpu.VMEM((4, 3, QB, 1024), BF16),
            pltpu.VMEM((8, GW, 256), BF16),
            pltpu.VMEM((8, GW, 256), BF16),
            pltpu.VMEM((2, 3, GW, 256), BF16),
            pltpu.VMEM((2, 3, GW, 256), BF16),
            pltpu.VMEM((GW, 256), BF16),
            pltpu.VMEM((GW, 256), BF16),
            pltpu.VMEM((4, 2, QB, QW), BF16),
            DMA((7,)),
            DMA, DMA,
            DMA((2,)), DMA((2,)),
            DMA((4, 3)), DMA((4, 3)),
            DMA((8,)), DMA((8,)),
            DMA((2, 3)), DMA((2, 3)),
            DMA, DMA,
        ],
        compiler_params=pltpu.CompilerParams(
            collective_id=2, has_side_effects=True, vmem_limit_bytes=58 * MIB
        ),
        name="finish",
    )(qg, own, other, inputs, w_query, w_key, w2, rope)


def shards(inputs, w_query, w_key, teacher_queries, teacher_keys, head_match, block_order):
    rope = rope_rows(block_order, lax.axis_index("sec"))
    picked_k, picked_q = pick(head_match, teacher_keys, teacher_queries)
    queries, keys, gotk, gotq, w2 = spread(picked_k, picked_q, inputs, w_query, w_key, rope)
    query_grads, own, other = attend(block_order, head_match, queries, keys, gotq, gotk, rope)
    rows, grad_query, grad_key = finish(
        query_grads.reshape(4, 2, QB, QW), own, other, inputs, w_query, w_key, w2, rope
    )
    return (rows[None], grad_query, grad_key)


def solution(mesh):
    return jax.shard_map(
        shards,
        mesh=mesh,
        in_specs=(
            P("seq", "sec", None),
            P(None, "head"),
            P(None, "head"),
            P("seq", "head", "sec"),
            P("seq", "head", "sec"),
            P(),
            P(),
        ),
        out_specs=(
            P("seq", ("sec", "head"), None),
            P(("sec", "seq"), "head"),
            P(("sec", "seq"), "head"),
        ),
        check_vma=False,
    )
```

time: 531 us -> 176 us (0.33)
  waiting for transfers between devices: 231 us -> 0 us
  Pallas kernels: 0 us -> 160 us
  matrix products: 86.4 us -> 0 us
  other arithmetic: 61.5 us -> 4.15 us
  blocking collectives: 56.9 us -> 0 us
  local copies, waits for them, and re-layouts: 61 us -> 10.4 us
  starting transfers between devices: 17.2 us -> 0 us
  between operations: 14 us -> 0.73 us
    reduce_scatter x3 -> x0, waiting for transfers between devices: 171 us -> none  [the longest x1 115 us: shards(): lax.psum_scatter((term + lax.dot_general(grad_keys, w_key, contract, pref...]
    pallas_call x0 -> x4, Pallas kernels: none -> 160 us  [the longest x1 67.4 us: finish(): pl.pallas_call(finish_kernel, out_shape=(jax.ShapeDtypeStruct((QB, D), BF...]
    dot_general x22 -> x0, matrix products: 86.4 us -> none  [the longest x4 13.3 us: one_head(): lax.dot_general(query, key_one, contract, preferred_element_type=jnp.floa...]
    all_to_all x2 -> x0, waiting for transfers between devices: 60.9 us -> none  [the longest x1 60.9 us: shards(): lax.all_to_all(sent_q, ('sec', 'head'), split_axis=0, concat_axis=0, tile...]
    all_gather x1 -> x0, blocking collectives: 56.9 us -> none  [shards(): all_keys = lax.all_gather(own_keys, 'sec', axis=1, tiled=True)]
    convert_element_type x5 -> x1, other arithmetic: 24.2 us -> 0.07 us  [rope_rows(): angles = positions.astype(F32)[:, None] * freqs[None, :]]
    reduce_sum x4 -> x0, other arithmetic: 22.4 us -> none  [masked_softmax(): return weights / jnp.sum(weights, axis=-1, keepdims=True)]
    gather x4 -> x0, local copies, waits for them, and re-layouts: 17.4 us -> none  [the longest x1 4.37 us: shards(): picked_q = jnp.take(local_q, local, axis=1).transpose(1, 0, 2)]
  transfers between devices with their start and end apart: 5 -> 0, of which waited for: 4 -> 0; matrix products, arithmetic and copies ran while one was open for 13% -> 0% of each run, Pallas kernels for 0% -> 0%
where the time goes in v1:
time: 176 us; the launch traced here: 175 us
  Pallas kernels  160 us (91%)
  local copies, waits for them, and re-layouts  10.4 us (6%)
  other arithmetic  4.15 us (2%)
    pallas_call x1, Pallas kernels, finish(): pl.pallas_call(finish_kernel, out_shape=(jax.ShapeDtypeStruct((QB, D), BF...  67.4 us
    pallas_call x1, Pallas kernels, spread(): pl.pallas_call(spread_kernel, out_shape=(jax.ShapeDtypeStruct((ROWS, QW),...  54 us
    pallas_call x1, Pallas kernels, attend(): pl.pallas_call(attend_kernel, out_shape=(jax.ShapeDtypeStruct((ROWS, QW),...  34.4 us
    unnamed x21, local copies, waits for them, and re-layouts  10.4 us
    pallas_call x1, Pallas kernels, pick(): pl.pallas_call(pick_kernel, out_shape=(jax.ShapeDtypeStruct(shape, BF16),...  3.66 us

profile of v1, /device:TPU:0, one launch (start us, length us, event | category | flops | bytes accessed | tf_op | source)
XLA Modules:
  0.0 174.8 jit_solution(15025283575907555676)
XLA Ops:
  0.6 0.7 dynamic-slice_multiply_fusion
  1.4 0.1 convert_bitcast_fusion
  1.5 1.9 %multiply_cosine_fusion = (f32[1024,64]{1,0:T(8,128)S(1)}, f32[1024,64]{1,0:T(8,128)S(1)}, f32[1024,64]{1,0:T(8,128)S(1)}) fusion(f32[64]{0:T(128)S(1)} %multiply_power_fusion, f32[1024]{0:T(1024)S(1)} %convert_bitcast_fusion), kind=kLoop, calls=%fused_computation.2 | loop fusion | flops 131072 | bytes 790784 | tf_op jit(solution)/shard_map/cos | solution.py:44
  3.4 0.3 maximum_bitcast_fusion
  3.7 1.1 pad_maximum_fusion.rope
  4.8 0.0 copy-start.1
  4.8 3.7 %pick.1 = (bf16[4,2,2,256,128]{4,3,2,1,0:T(8,128)(2,1)}, bf16[4,2,2,256,128]{4,3,2,1,0:T(8,128)(2,1)}) custom-call(s32[32]{0:T(128)} %match_ref.3, bf16[1,256,8192]{2,1,0:T(8,128)(2,1)} %tk_ref.1, bf16[1,256,8192]{2,1,0:T(8,128)(2,1)} %tq_ref.1), custom_call_target="tpu_custom_call" | custom-call | tf_op jit(solution)/shard_map/pick/pallas_call | solution.py:86
  8.5 0.0 copy-done.1
  8.5 0.0 copy-start.2
  8.5 1.2 copy-done.2
  9.7 0.0 copy-start.3
  9.7 1.2 copy-done.3
  10.9 0.0 copy-start
  10.9 0.0 copy-start.7
  10.9 0.0 copy-start.8
  10.9 54.0 %spread.1 = (bf16[1024,512]{1,0:T(8,128)(2,1)S(1)}, bf16[2048,128]{1,0:T(8,128)(2,1)S(1)}, bf16[2,2,2048,128]{3,2,1,0:T(8,128)(2,1)}, bf16[2,2,1024,128]{3,2,1,0:T(8,128)(2,1)S(1)}, bf16[4096,640]{1,0:T(8,128)(2,1)}) custom-call(bf16[4,2,2,256,128]{4,3,2,1,0:T(8,128)(2,1)S(1)} %copy-done.2, bf16[4,2,2,256,128]{4,3,2,1,0:T(8,128)(2,1)S(1)} %copy-done.3, ...), custom_call_target="tpu_custom_call" | custom-call | tf_op jit(solution)/shard_map/spread/pallas_call | solution.py:328
  65.0 0.0 copy-done
  65.0 0.0 copy-done.7
  65.0 0.0 copy-done.8
  65.0 34.4 %attend.1 = (bf16[1024,512]{1,0:T(8,128)(2,1)S(1)}, f32[1024,128]{1,0:T(8,128)S(1)}, bf16[1024,128]{1,0:T(8,128)(2,1)S(1)}) custom-call(s32[16]{0:T(128)S(1)} %copy-done.8, s32[32]{0:T(128)S(1)} %copy-done.7, bf16[1024,512]{1,0:T(8,128)(2,1)S(1)} %get-tuple-element.18.q_ref, bf16[2048,128]{1,0:T(8,128)(2,1)S(1)} %get-tuple-element.19.keys, ...), custom_call_target="tpu_custom_call" | custom-call | tf_op jit(solution)/shard_map/attend/pallas_call | solution.py:469
  99.5 0.0 copy-start.4
  99.5 1.0 copy-done.4
  100.4 0.0 copy-start.5
  100.4 0.8 copy-done.5
  101.2 0.0 copy-start.6
  101.2 0.7 copy-done.6
  101.9 67.4 %finish.1 = (bf16[128,4096]{1,0:T(8,128)(2,1)}, bf16[256,512]{1,0:T(8,128)(2,1)}, bf16[256,128]{1,0:T(8,128)(2,1)}) custom-call(bf16[4,2,128,512]{3,2,1,0:T(8,128)(2,1)} %bitcast.8, f32[1024,128]{1,0:T(8,128)} %copy-done.5, bf16[1024,128]{1,0:T(8,128)(2,1)} %copy-done.6, bf16[1,1024,4096]{2,1,0:T(8,128)(2,1)} %tok.3, bf16[4096,512]{1,0:T(8,128)(2,1)} %wq.3, ...), custom_call_target="tpu_custom_call" | custom-call | tf_op jit(solution)/shard_map/finish/pallas_call | solution.py:658
  169.3 2.3 %copy.13 = bf16[1,128,4096]{2,1,0:T(8,128)(2,1)} copy(bf16[1,128,4096]{2,1,0:T(8,128)(2,1)} %bitcast.9) | data formatting | bytes 2097152
  171.6 1.7 copy.14
  173.3 1.5 copy.15
  (1 shorter events, 0.0 us)
Async XLA Ops:
  4.8 3.7 %copy-start.1 = (bf16[4096,128]{1,0:T(8,128)(2,1)S(1)}, bf16[4096,128]{1,0:T(8,128)(2,1)}, u32[]{:S(2)}) copy-start(bf16[4096,128]{1,0:T(8,128)(2,1)} %wk.3) | copy-start | bytes 3145732
  8.5 1.2 copy-start.2
  9.7 1.2 copy-start.3
  10.9 54.1 %copy-start = (f32[2,1024,128]{2,1,0:T(8,128)S(1)}, f32[2,1024,128]{2,1,0:T(8,128)}, u32[]{:S(2)}) copy-start(f32[2,1024,128]{2,1,0:T(8,128)} %pad_maximum_fusion.rope) | copy-start | bytes 3145732
  10.9 54.1 %copy-start.7 = (s32[32]{0:T(128)S(1)}, s32[32]{0:T(128)}, u32[]{:S(2)}) copy-start(s32[32]{0:T(128)} %match_ref.3) | copy-start | bytes 388
  10.9 54.1 %copy-start.8 = (s32[16]{0:T(128)S(1)}, s32[16]{0:T(128)}, u32[]{:S(2)}) copy-start(s32[16]{0:T(128)} %order_ref.1) | copy-start | bytes 196
  99.5 1.0 copy-start.4
  100.4 0.8 copy-start.5
  101.2 0.7 copy-start.6

commit v2 on v1

--- a/solution.py
+++ b/solution.py
@@ -22,6 +22,7 @@
 QW = 512
 CK = 256
 MIB = 1024 * 1024
+LOWEST = -1e30
 
 rope_base = 500000.0
 grad_scale = 16.0
@@ -35,21 +36,6 @@
 BF16 = jnp.bfloat16
 
 
-def rope_rows(block_order, sec):
-    own = lax.dynamic_slice_in_dim(block_order, sec * HALF_BLKS, HALF_BLKS, 0)
-    positions = (own[:, None] * QB + jnp.arange(QB, dtype=jnp.int32)[None, :]).reshape(-1)
-    half = HD // 2
-    freqs = rope_base ** (-(jnp.arange(half, dtype=F32) * 2.0) / HD)
-    angles = positions.astype(F32)[:, None] * freqs[None, :]
-    cosine, sine = jnp.cos(angles), jnp.sin(angles)
-    return jnp.stack(
-        [
-            jnp.concatenate([cosine, cosine], axis=1),
-            jnp.concatenate([-sine, sine], axis=1),
-        ]
-    )
-
-
 def section_slots(match_ref, group, section):
     low, high = jnp.int32(TH_SEC - 1), jnp.int32(0)
     for i in range(HEADS):
@@ -60,7 +46,9 @@
     return low, high
 
 
-def pick_kernel(match_ref, tk_ref, tq_ref, k_out, q_out, k_v, q_v, in_sems, out_sems):
+def pick_kernel(
+    match_ref, order_ref, freqs, tk_ref, tq_ref, k_out, q_out, rope, k_v, q_v, in_sems, out_sems
+):
     sec = lax.axis_index("sec")
     copies = []
     for g in range(GROUPS):
@@ -74,6 +62,19 @@
                     place, dst.at[g // 2, g % 2, j], out_sems.at[a, g * 2 + j]
                 )
                 copies.append((load, store))
+    lane = lax.broadcasted_iota(jnp.int32, (QB, HD), 1)
+    offset = lax.broadcasted_iota(jnp.int32, (QB, HD), 0)
+
+    def one_block(b, _):
+        position = order_ref[sec * HALF_BLKS + b] * QB + offset
+        angles = position.astype(F32) * freqs[...]
+        at = pl.ds(pl.multiple_of(b * QB, QB), QB)
+        sine = jnp.sin(angles)
+        rope[0, at, :] = jnp.cos(angles)
+        rope[1, at, :] = jnp.where(lane < HD // 2, -sine, sine)
+        return 0
+
+    lax.fori_loop(0, HALF_BLKS, one_block, 0)
     for load, store in copies:
         load.wait()
         store.start()
@@ -81,21 +82,29 @@
         store.wait()
 
 
-def pick(match, teacher_keys, teacher_queries):
+def pick(match, order, teacher_keys, teacher_queries):
+    half = HD // 2
+    freqs = rope_base ** (-(jnp.arange(half, dtype=F32) * 2.0) / HD)
+    freqs = jnp.concatenate([freqs, freqs])[None]
     shape = (4, 2, 2, TROWS, HD)
     return pl.pallas_call(
         pick_kernel,
-        out_shape=(jax.ShapeDtypeStruct(shape, BF16), jax.ShapeDtypeStruct(shape, BF16)),
-        in_specs=[SMEM, ANY, ANY],
-        out_specs=(ANY, ANY),
+        out_shape=(
+            jax.ShapeDtypeStruct(shape, BF16),
+            jax.ShapeDtypeStruct(shape, BF16),
+            jax.ShapeDtypeStruct((2, ROWS, HD), F32),
+        ),
+        in_specs=[SMEM, SMEM, VMEM, ANY, ANY],
+        out_specs=(ANY, ANY, VMEM),
         scratch_shapes=[
             pltpu.VMEM(shape, BF16),
             pltpu.VMEM(shape, BF16),
             DMA((2, 16)),
             DMA((2, 16)),
         ],
+        compiler_params=pltpu.CompilerParams(vmem_limit_bytes=63 * MIB),
         name="pick",
-    )(match, teacher_keys, teacher_queries)
+    )(match, order, freqs, teacher_keys, teacher_queries)
 
 
 def spread_kernel(
@@ -144,13 +153,14 @@
         pl.semaphore_signal(barrier, inc=1, device_id=where, device_id_type=MESH)
     pl.semaphore_wait(barrier, len(greet))
 
-    zcopies = []
+    def along_z(a, d):
+        src, dst = ((sk, zk), (sq, zq))[a]
+        return send(
+            src.at[(z + d) % 4], dst.at[d - 1], zs.at[a, d - 1], zr.at[a, d - 1], depth(d)
+        )
+
     for d in (1, 3, 2):
-        to = (z + d) % 4
-        for a, (src, dst) in enumerate(((sk, zk), (sq, zq))):
-            copy = send(src.at[to], dst.at[d - 1], zs.at[a, d - 1], zr.at[a, d - 1], depth(d))
-            copy.start()
-            zcopies.append(copy)
+        along_z(0, d).start()
 
     def krows(d, xhs):
         return pl.ds(pl.multiple_of((((z + 4 - d) % 4) * 2 + xhs) * TROWS, TROWS), TROWS)
@@ -181,18 +191,20 @@
             half=half,
         )
 
-    def start_x(d):
+    def start_keys(d):
         m = along_x(d)
         m["ck"].start()
         m["pk"].start()
+        m["lk"].start()
+
+    def start_queries(d):
+        m = along_x(d)
         m["qx"].start()
 
         @pl.when(m["half"] != sec)
         def _():
             m["qp"].start()
 
-        m["lk"].start()
-
         @pl.when(m["half"] == sec)
         def _():
             m["lq"].start()
@@ -201,7 +213,8 @@
         got = gotk.at[1 - sec, :, krows(d, 1 - xh)]
         return send(got, got, rks.at[d], rkr.at[d], partner)
 
-    start_x(0)
+    start_keys(0)
+    start_queries(0)
 
     for load in loads:
         load.wait()
@@ -246,11 +259,12 @@
         copy.start()
         relays.append(copy)
 
+    for d in (1, 3, 2):
+        along_z(1, d).start()
     wait_relay(0)
     for d in (1, 3):
-        zcopies[0 if d == 1 else 2].wait_recv()
-        zcopies[1 if d == 1 else 3].wait_recv()
-        start_x(d)
+        along_z(0, d).wait_recv()
+        start_keys(d)
 
     wcopies = []
 
@@ -271,9 +285,11 @@
         forward(y, j, wcs, wcr, j, core)
     wait_relay(1)
     wait_relay(3)
-    zcopies[4].wait_recv()
-    zcopies[5].wait_recv()
-    start_x(2)
+    along_z(0, 2).wait_recv()
+    start_keys(2)
+    for d in (1, 3):
+        along_z(1, d).wait_recv()
+        start_queries(d)
     wait_piece(y + 3, c, 0, wys.at[0], wyr.at[0])
     forward(y + 3, 0, wrs, wrr, 0, up)
     forward(y + 3, 0, wcs, wcr, 2, core)
@@ -281,6 +297,8 @@
     forward(y + 1, 1, wrs, wrr, 1, down)
     forward(y + 1, 1, wcs, wcr, 3, core)
     wait_relay(2)
+    along_z(1, 2).wait_recv()
+    start_queries(2)
     wait_piece(y + 3, c, 1, wys.at[1], wyr.at[1])
     forward(y + 3, 1, wcs, wcr, 4, core)
     wait_piece(y + 1, c, 0, wys.at[2], wyr.at[2])
@@ -320,7 +338,10 @@
         m["qx"].wait_send()
     key_own.wait()
     key_send.wait_send()
-    for copy in zcopies + first + relays + wcopies:
+    for d in (1, 3, 2):
+        for a in range(2):
+            along_z(a, d).wait_send()
+    for copy in first + relays + wcopies:
         copy.wait_send()
 
 
@@ -358,7 +379,7 @@
             DMA((8,)), DMA((8,)),
         ],
         compiler_params=pltpu.CompilerParams(
-            collective_id=1, has_side_effects=True, vmem_limit_bytes=48 * MIB
+            collective_id=1, has_side_effects=True, vmem_limit_bytes=63 * MIB
         ),
         name="spread",
     )(picked_k, picked_q, inputs, w_query, w_key, rope)
@@ -367,7 +388,7 @@
 def attend_kernel(
     order_ref, match_ref, q_ref, keys, gotq, gotk, rope,
     qg_ref, own_ref, other_ref,
-    kp, tkp, tqv, st, g_acc, dk, sems, qsems,
+    kp, tkp, tqv, st, ms, g_acc, dk, sems, qsems,
 ):
     sec, head = lax.axis_index("sec"), lax.axis_index("head")
     exponent = scale * math.log2(math.e)
@@ -408,42 +429,50 @@
             [q_ref[rows, i * HD : (i + 1) * HD] for i in range(HEADS)], axis=0
         )
 
-        def scores(chunk, top, masked):
+        def scores(chunk, carry, masked):
             at = pl.ds(pl.multiple_of(chunk * CK, CK), CK)
-            student = lax.dot_general(kp[at, :], queries, nt, preferred_element_type=F32)
-            teacher = jnp.concatenate(
-                [
-                    lax.dot_general(tkp[i, at, :], tqv[i, rows, :], nt, preferred_element_type=F32)
-                    for i in range(HEADS)
-                ],
-                axis=1,
-            )
-            both = jnp.concatenate([student, teacher], axis=1)
-            if masked:
-                key_at = lax.broadcasted_iota(jnp.int32, both.shape, 0) + chunk * CK
-                row_at = lax.broadcasted_iota(jnp.int32, both.shape, 1) % QB + block * QB
-                both = jnp.where(key_at <= row_at, both, -jnp.inf)
-            st[at, :] = both
-            return jnp.maximum(top, jnp.max(both.reshape(CK // 8, 8, 2 * QW), axis=0))
-
-        top = jnp.full((8, 2 * QW), -jnp.inf, F32)
-        top = lax.fori_loop(0, last, lambda chunk, t: scores(chunk, t, False), top)
-        top = scores(last, top, True)
-        top = jnp.max(top, axis=0, keepdims=True)
-
-        def weights(chunk, total):
-            at = pl.ds(pl.multiple_of(chunk * CK, CK), CK)
-            e = jnp.exp2((st[at, :] - top) * exponent)
-            st[at, :] = e
-            return total + jnp.sum(e.reshape(CK // 8, 8, 2 * QW), axis=0)
-
-        total = lax.fori_loop(0, last + 1, weights, jnp.zeros((8, 2 * QW), F32))
-        inverse = grad_scale / jnp.sum(total, axis=0, keepdims=True)
+            tops, totals = [], []
+            for unit in range(6):
+                if unit < 2:
+                    columns = slice(unit * 256, unit * 256 + 256)
+                    part = lax.dot_general(
+                        kp[at, :], queries[columns], nt, preferred_element_type=F32
+                    )
+                else:
+                    i = unit - 2
+                    columns = slice(QW + i * HD, QW + (i + 1) * HD)
+                    part = lax.dot_general(
+                        tkp[i, at, :], tqv[i, rows, :], nt, preferred_element_type=F32
+                    )
+                if masked:
+                    key_at = lax.broadcasted_iota(jnp.int32, part.shape, 0) + chunk * CK
+                    row_at = lax.broadcasted_iota(jnp.int32, part.shape, 1) % QB + block * QB
+                    part = jnp.where(key_at <= row_at, part, LOWEST)
+                part = part.reshape(CK // 8, 8, part.shape[1])
+                before, total = carry[0][:, columns], carry[1][:, columns]
+                top = jnp.maximum(before, jnp.max(part, axis=0))
+                part = jnp.exp2((part - top[None]) * exponent)
+                st[at, columns] = part.reshape(CK, part.shape[2])
+                tops.append(top)
+                totals.append(total * jnp.exp2((before - top) * exponent) + jnp.sum(part, axis=0))
+            tops, totals = jnp.concatenate(tops, axis=1), jnp.concatenate(totals, axis=1)
+            ms[chunk] = tops
+            return tops, totals
+
+        carry = (jnp.full((8, 2 * QW), LOWEST, F32), jnp.zeros((8, 2 * QW), F32))
+        carry = lax.fori_loop(0, last, lambda chunk, t: scores(chunk, t, False), carry)
+        tops, totals = scores(last, carry, True)
+        top = jnp.max(tops, axis=0, keepdims=True)
+        totals = totals * jnp.exp2((tops - top) * exponent)
+        inverse = grad_scale / jnp.sum(totals, axis=0, keepdims=True)
         g_acc[...] = jnp.zeros_like(g_acc)
 
         def grads(chunk, _):
             at = pl.ds(pl.multiple_of(chunk * CK, CK), CK)
-            g = (st[at, :QW] * inverse[:, :QW] - st[at, QW:] * inverse[:, QW:]).astype(BF16)
+            factor = jnp.exp2((ms[chunk] - top) * exponent) * inverse
+            both = st[at, :].reshape(CK // 8, 8, 2 * QW)
+            g = both[:, :, :QW] * factor[None, :, :QW] - both[:, :, QW:] * factor[None, :, QW:]
+            g = g.reshape(CK, QW).astype(BF16)
             dk[at, :] += jnp.dot(g, queries, preferred_element_type=F32)
             g_acc[...] += lax.dot_general(g, kp[at, :], tn, preferred_element_type=F32)
             return 0
@@ -480,12 +509,13 @@
             pltpu.VMEM((HEADS, LEN, HD), BF16),
             pltpu.VMEM((HEADS, ROWS, HD), BF16),
             pltpu.VMEM((LEN, 2 * QW), F32),
+            pltpu.VMEM((LEN // CK, 8, 2 * QW), F32),
             pltpu.VMEM((QW, HD), F32),
             pltpu.VMEM((LEN, HD), F32),
             DMA((HEADS + 1, NBLK)),
             DMA((HEADS,)),
         ],
-        compiler_params=pltpu.CompilerParams(vmem_limit_bytes=48 * MIB),
+        compiler_params=pltpu.CompilerParams(vmem_limit_bytes=63 * MIB),
         name="attend",
     )(order, match, queries, keys, gotq, gotk, rope)
 
@@ -533,8 +563,14 @@
 
     key_send = send(other, key_rx, key_s, key_r, partner)
     key_send.start()
-    q_send = send(qg.at[:, 1 - xh], g2, x_s.at[0], x_r.at[0], far)
-    q_send.start()
+
+    def far_copy(a, r):
+        zz = (z + r) % 4
+        src, dst = ((qg, g2), (gk_v, k2))[a]
+        return send(src.at[zz, 1 - xh], dst.at[zz], x_s.at[a, r], x_r.at[a, r], far)
+
+    for r in (3, 1):
+        far_copy(0, r).start()
     loads[0].wait()
     for b in range(HALF_BLKS):
         gt[0:QW, b * QB : (b + 1) * QB] = qg_v[b // 2, b % 2].T
@@ -548,8 +584,10 @@
         total = total.astype(BF16)
         gk_v[b // 2, b % 2] = total
         gt[QW:GW, b * QB : (b + 1) * QB] = total.T
-    k_send = send(gk_v.at[:, 1 - xh], k2, x_s.at[1], x_r.at[1], far)
-    k_send.start()
+    for r in (3, 1, 2, 0):
+        far_copy(1, r).start()
+    for r in (2, 0):
+        far_copy(0, r).start()
 
     def weight_part(s, yy, cc):
         start = (s * 8 + (yy % 4) * 2 + cc) * 256
@@ -572,8 +610,6 @@
     lax.fori_loop(0, 8, to_core, 0)
     for load in loads[2:]:
         load.wait()
-    q_send.wait_recv()
-    k_send.wait_recv()
 
     nt = (((1,), (1,)), ((), ()))
 
@@ -593,6 +629,9 @@
         )
 
     def z_step(step):
+        for r in {0: (3, 1), 1: (2,), 2: (), 3: (0,)}[step]:
+            far_copy(0, r).wait_recv()
+            far_copy(1, r).wait_recv()
         for stream in (0, 2, 1, 3):
             target = z + 3 - step if stream < 2 else z + 1 + step
             term = row_term(target, stream * 1024)
@@ -643,8 +682,11 @@
     gq_out[...] = keep[:, :QW].astype(BF16)
     gk_out[...] = keep[:, QW:].astype(BF16)
 
-    for copy in (key_send, q_send, k_send, sec_copy):
+    for copy in (key_send, sec_copy):
         copy.wait_send()
+    for r in range(4):
+        far_copy(0, r).wait_send()
+        far_copy(1, r).wait_send()
     for i in range(8):
         core_copy(i).wait_send()
     for step in range(3):
@@ -686,28 +728,60 @@
             pltpu.VMEM((4, 2, QB, QW), BF16),
             DMA((7,)),
             DMA, DMA,
-            DMA((2,)), DMA((2,)),
+            DMA((2, 4)), DMA((2, 4)),
             DMA((4, 3)), DMA((4, 3)),
             DMA((8,)), DMA((8,)),
             DMA((2, 3)), DMA((2, 3)),
             DMA, DMA,
         ],
         compiler_params=pltpu.CompilerParams(
-            collective_id=2, has_side_effects=True, vmem_limit_bytes=58 * MIB
+            collective_id=2, has_side_effects=True, vmem_limit_bytes=63 * MIB
         ),
         name="finish",
     )(qg, own, other, inputs, w_query, w_key, w2, rope)
 
 
+def close_kernel(rows, gq, gk, rows_out, gq_out, gk_out, rows_v, gq_v, gk_v, sems):
+    triples = [(gk, gk_v, gk_out), (gq, gq_v, gq_out)]
+    for part in range(4):
+        at = pl.ds(part * 32, 32)
+        triples.append((rows.at[at], rows_v.at[at], rows_out.at[0, at]))
+    loads = [pltpu.make_async_copy(a, b, sems.at[0, i]) for i, (a, b, _) in enumerate(triples)]
+    stores = [pltpu.make_async_copy(b, c, sems.at[1, i]) for i, (_, b, c) in enumerate(triples)]
+    for load in loads:
+        load.start()
+    for load, store in zip(loads, stores):
+        load.wait()
+        store.start()
+    for store in stores:
+        store.wait()
+
+
+def close(rows, grad_query, grad_key):
+    held = [pltpu.VMEM(x.shape, x.dtype) for x in (rows, grad_query, grad_key)]
+    return pl.pallas_call(
+        close_kernel,
+        out_shape=(
+            jax.ShapeDtypeStruct((1,) + rows.shape, rows.dtype),
+            jax.ShapeDtypeStruct(grad_query.shape, grad_query.dtype),
+            jax.ShapeDtypeStruct(grad_key.shape, grad_key.dtype),
+        ),
+        in_specs=[ANY] * 3,
+        out_specs=(ANY,) * 3,
+        scratch_shapes=[*held, DMA((2, 6))],
+        compiler_params=pltpu.CompilerParams(vmem_limit_bytes=63 * MIB),
+        name="close",
+    )(rows, grad_query, grad_key)
+
+
 def shards(inputs, w_query, w_key, teacher_queries, teacher_keys, head_match, block_order):
-    rope = rope_rows(block_order, lax.axis_index("sec"))
-    picked_k, picked_q = pick(head_match, teacher_keys, teacher_queries)
+    picked_k, picked_q, rope = pick(head_match, block_order, teacher_keys, teacher_queries)
     queries, keys, gotk, gotq, w2 = spread(picked_k, picked_q, inputs, w_query, w_key, rope)
     query_grads, own, other = attend(block_order, head_match, queries, keys, gotq, gotk, rope)
     rows, grad_query, grad_key = finish(
         query_grads.reshape(4, 2, QB, QW), own, other, inputs, w_query, w_key, w2, rope
     )
-    return (rows[None], grad_query, grad_key)
+    return close(rows, grad_query, grad_key)
 
 
 def solution(mesh):

time: 176 us -> 167 us (0.949)
  local copies, waits for them, and re-layouts: 10.4 us -> 0 us
  Pallas kernels: 160 us -> 165 us
  other arithmetic: 4.15 us -> 0.6 us
    unnamed x21 -> x0, local copies, waits for them, and re-layouts: 10.4 us -> none
    pallas_call x1, Pallas kernels: 67.4 us -> 72.8 us  [finish(): pl.pallas_call(finish_kernel, out_shape=(jax.ShapeDtypeStruct((QB, D), BF...]
    pallas_call x1, Pallas kernels: 34.4 us -> 29 us  [attend(): pl.pallas_call(attend_kernel, out_shape=(jax.ShapeDtypeStruct((ROWS, QW),...]
    pallas_call x0 -> x1, Pallas kernels: none -> 2.14 us  [close(): pl.pallas_call(close_kernel, out_shape=(jax.ShapeDtypeStruct((1,) + rows....]
    pallas_call x1, Pallas kernels: 3.66 us -> 5.77 us  [pick(): pl.pallas_call(pick_kernel, out_shape=(jax.ShapeDtypeStruct(shape, BF16),...]
    cos x1 -> x0, other arithmetic: 1.91 us -> none  [rope_rows(): cosine, sine = (jnp.cos(angles), jnp.sin(angles))]
where the time goes in v2:
time: 167 us
  Pallas kernels  165 us (99%)
    pallas_call x1, Pallas kernels, finish(): pl.pallas_call(finish_kernel, out_shape=(jax.ShapeDtypeStruct((QB, D), BF...  72.8 us
    pallas_call x1, Pallas kernels, spread(): pl.pallas_call(spread_kernel, out_shape=(jax.ShapeDtypeStruct((ROWS, QW),...  55.7 us
    pallas_call x1, Pallas kernels, attend(): pl.pallas_call(attend_kernel, out_shape=(jax.ShapeDtypeStruct((ROWS, QW),...  29 us
    pallas_call x1, Pallas kernels, pick(): pl.pallas_call(pick_kernel, out_shape=(jax.ShapeDtypeStruct(shape, BF16),...  5.77 us

profile of v2, /device:TPU:0, one launch (start us, length us, event | category | flops | bytes accessed | tf_op | source)
XLA Modules:
  0.0 166.9 jit_solution(6487963234083300852)
XLA Ops:
  0.6 0.6 maximum_bitcast_fusion.freqs
  1.2 5.8 %pick.1 = (bf16[4,2,2,256,128]{4,3,2,1,0:T(8,128)(2,1)}, bf16[4,2,2,256,128]{4,3,2,1,0:T(8,128)(2,1)}, f32[2,1024,128]{2,1,0:T(8,128)}) custom-call(s32[32]{0:T(128)} %match_ref.3, s32[16]{0:T(128)} %order_ref.3, f32[1,128]{1,0:T(1,128)} %maximum_bitcast_fusion.freqs, bf16[1,256,8192]{2,1,0:T(8,128)(2,1)} %tk_ref.1, bf16[1,256,8192]{2,1,0:T(8,128)(2,1)} %tq_ref.1), custom_call_target="tpu_custom_call" | custom-call | tf_op jit(solution)/shard_map/pick/pallas_call | solution.py:90
  7.0 55.7 %spread.1 = (bf16[1024,512]{1,0:T(8,128)(2,1)}, bf16[2048,128]{1,0:T(8,128)(2,1)}, bf16[2,2,2048,128]{3,2,1,0:T(8,128)(2,1)}, bf16[2,2,1024,128]{3,2,1,0:T(8,128)(2,1)}, bf16[4096,640]{1,0:T(8,128)(2,1)}) custom-call(bf16[4,2,2,256,128]{4,3,2,1,0:T(8,128)(2,1)} %get-tuple-element.17.sk, bf16[4,2,2,256,128]{4,3,2,1,0:T(8,128)(2,1)} %get-tuple-element.18.sq, ...), custom_call_target="tpu_custom_call" | custom-call | tf_op jit(solution)/shard_map/spread/pallas_call | solution.py:349
  62.7 29.0 %attend.1 = (bf16[1024,512]{1,0:T(8,128)(2,1)}, f32[1024,128]{1,0:T(8,128)}, bf16[1024,128]{1,0:T(8,128)(2,1)}) custom-call(s32[16]{0:T(128)} %order_ref.3, s32[32]{0:T(128)} %match_ref.3, bf16[1024,512]{1,0:T(8,128)(2,1)} %get-tuple-element.20.q_ref, bf16[2048,128]{1,0:T(8,128)(2,1)} %get-tuple-element.21.keys, ...), custom_call_target="tpu_custom_call" | custom-call | tf_op jit(solution)/shard_map/attend/pallas_call | solution.py:498
  91.7 72.8 %finish.1 = (bf16[128,4096]{1,0:T(8,128)(2,1)}, bf16[256,512]{1,0:T(8,128)(2,1)}, bf16[256,128]{1,0:T(8,128)(2,1)}) custom-call(bf16[4,2,128,512]{3,2,1,0:T(8,128)(2,1)} %bitcast.3, f32[1024,128]{1,0:T(8,128)} %get-tuple-element.25.own, bf16[1024,128]{1,0:T(8,128)(2,1)} %get-tuple-element.26.other, bf16[1,1024,4096]{2,1,0:T(8,128)(2,1)} %tok.3, ...), custom_call_target="tpu_custom_call" | custom-call | tf_op jit(solution)/shard_map/finish/pallas_call | solution.py:700
  164.6 2.1 %close.1 = (bf16[1,128,4096]{2,1,0:T(8,128)(2,1)}, bf16[256,512]{1,0:T(8,128)(2,1)}, bf16[256,128]{1,0:T(8,128)(2,1)}) custom-call(bf16[128,4096]{1,0:T(8,128)(2,1)} %get-tuple-element.28.rows, bf16[256,512]{1,0:T(8,128)(2,1)} %get-tuple-element.29.gq, bf16[256,128]{1,0:T(8,128)(2,1)} %get-tuple-element.30.gk), custom_call_target="tpu_custom_call" | custom-call | tf_op jit(solution)/shard_map/close/pallas_call | solution.py:762
  (1 shorter events, 0.0 us)

commit v3 on v2

--- a/solution.py
+++ b/solution.py
@@ -2,6 +2,7 @@
 
 import jax
 import jax.numpy as jnp
+import numpy as np
 from jax import lax
 from jax.experimental import pallas as pl
 from jax.experimental.pallas import tpu as pltpu
@@ -20,7 +21,7 @@
 D = 4096
 GW = 640
 QW = 512
-CK = 256
+CK = 512
 MIB = 1024 * 1024
 LOWEST = -1e30
 
@@ -46,9 +47,7 @@
     return low, high
 
 
-def pick_kernel(
-    match_ref, order_ref, freqs, tk_ref, tq_ref, k_out, q_out, rope, k_v, q_v, in_sems, out_sems
-):
+def pick_kernel(match_ref, tk_ref, tq_ref, k_out, q_out, k_v, q_v, in_sems, out_sems):
     sec = lax.axis_index("sec")
     copies = []
     for g in range(GROUPS):
@@ -62,19 +61,6 @@
                     place, dst.at[g // 2, g % 2, j], out_sems.at[a, g * 2 + j]
                 )
                 copies.append((load, store))
-    lane = lax.broadcasted_iota(jnp.int32, (QB, HD), 1)
-    offset = lax.broadcasted_iota(jnp.int32, (QB, HD), 0)
-
-    def one_block(b, _):
-        position = order_ref[sec * HALF_BLKS + b] * QB + offset
-        angles = position.astype(F32) * freqs[...]
-        at = pl.ds(pl.multiple_of(b * QB, QB), QB)
-        sine = jnp.sin(angles)
-        rope[0, at, :] = jnp.cos(angles)
-        rope[1, at, :] = jnp.where(lane < HD // 2, -sine, sine)
-        return 0
-
-    lax.fori_loop(0, HALF_BLKS, one_block, 0)
     for load, store in copies:
         load.wait()
         store.start()
@@ -82,20 +68,16 @@
         store.wait()
 
 
-def pick(match, order, teacher_keys, teacher_queries):
-    half = HD // 2
-    freqs = rope_base ** (-(jnp.arange(half, dtype=F32) * 2.0) / HD)
-    freqs = jnp.concatenate([freqs, freqs])[None]
+def pick(match, teacher_keys, teacher_queries):
     shape = (4, 2, 2, TROWS, HD)
     return pl.pallas_call(
         pick_kernel,
         out_shape=(
             jax.ShapeDtypeStruct(shape, BF16),
             jax.ShapeDtypeStruct(shape, BF16),
-            jax.ShapeDtypeStruct((2, ROWS, HD), F32),
         ),
-        in_specs=[SMEM, SMEM, VMEM, ANY, ANY],
-        out_specs=(ANY, ANY, VMEM),
+        in_specs=[SMEM, ANY, ANY],
+        out_specs=(ANY, ANY),
         scratch_shapes=[
             pltpu.VMEM(shape, BF16),
             pltpu.VMEM(shape, BF16),
@@ -104,13 +86,13 @@
         ],
         compiler_params=pltpu.CompilerParams(vmem_limit_bytes=63 * MIB),
         name="pick",
-    )(match, order, freqs, teacher_keys, teacher_queries)
+    )(match, teacher_keys, teacher_queries)
 
 
 def spread_kernel(
-    sk, sq, tok, wq, wk, rope,
-    q_out, keys_out, gotk, gotq, w2,
-    rope_v, tok_v, w_v, k_v, zk, zq,
+    sk, sq, tok, wq, wk, order_ref, freqs,
+    q_out, keys_out, gotk, gotq, w2, rope_v,
+    tok_v, w_v, k_v, zk, zq,
     load_sem, own_sem, zs, zr, pks, pkr, cks, ckr, rks, rkr, qps, qpr, qxs, qxr,
     keys_s, keys_r, w1s, w1r, wys, wyr, wrs, wrr, wcs, wcr,
 ):
@@ -135,7 +117,6 @@
     loads = [
         pltpu.make_async_copy(wq, w_v.at[:, pl.ds(0, QW)], load_sem.at[4]),
         pltpu.make_async_copy(wk, w_v.at[:, pl.ds(QW, HD)], load_sem.at[5]),
-        pltpu.make_async_copy(rope, rope_v, load_sem.at[6]),
     ]
     for load in loads:
         load.start()
@@ -216,6 +197,16 @@
     start_keys(0)
     start_queries(0)
 
+    def rope_block(b, _):
+        lane = lax.broadcasted_iota(jnp.int32, (QB, HD), 1)
+        offset = lax.broadcasted_iota(jnp.int32, (QB, HD), 0)
+        angles = (order_ref[sec * HALF_BLKS + b] * QB + offset).astype(F32) * freqs[...]
+        at = pl.ds(pl.multiple_of(b * QB, QB), QB)
+        sine = jnp.sin(angles)
+        rope_v[0, at, :] = jnp.cos(angles)
+        rope_v[1, at, :] = jnp.where(lane < HD // 2, -sine, sine)
+        return 0
+
     for load in loads:
         load.wait()
 
@@ -224,10 +215,14 @@
         return ref.at[pl.ds(pl.multiple_of(start, 256), 256)]
 
     first = []
-    for j in range(2):
+
+    def send_piece(j):
         copy = send(piece(w_v, y, c, j), piece(w2, y, c, j), w1s.at[j], w1r.at[j], cross)
         copy.start()
         first.append(copy)
+
+    send_piece(0)
+    lax.fori_loop(0, HALF_BLKS, rope_block, 0)
 
     def project(r, _):
         token_load(r).wait()
@@ -243,13 +238,6 @@
                 k_v[rows, :] = part
         return 0
 
-    lax.fori_loop(0, 4, project, 0)
-    key_rows = keys_out.at[pl.ds(pl.multiple_of(sec * ROWS, ROWS), ROWS)]
-    key_send = send(k_v, key_rows, keys_s, keys_r, partner)
-    key_send.start()
-    key_own = pltpu.make_async_copy(k_v, key_rows, own_sem.at[2, 0])
-    key_own.start()
-
     relays = []
 
     def wait_relay(d):
@@ -259,13 +247,6 @@
         copy.start()
         relays.append(copy)
 
-    for d in (1, 3, 2):
-        along_z(1, d).start()
-    wait_relay(0)
-    for d in (1, 3):
-        along_z(0, d).wait_recv()
-        start_keys(d)
-
     wcopies = []
 
     def forward(src_y, j, sems, rsems, index, where):
@@ -278,18 +259,38 @@
         ref = piece(w2, src_y, cc, j)
         send(ref, ref, sem, rsem, core).wait_recv()
 
-    for j in range(2):
+    def spread_piece(j):
         wait_piece(y, c, j, w1s.at[j], w1r.at[j])
         forward(y, j, wys, wyr, j, up)
         forward(y, j, wys, wyr, 2 + j, down)
         forward(y, j, wcs, wcr, j, core)
+
+    lax.fori_loop(0, 1, project, 0)
+    for d in (1, 3, 2):
+        along_z(1, d).start()
+    lax.fori_loop(1, 2, project, 0)
+    wait_relay(0)
+    for d in (1, 3):
+        along_z(0, d).wait_recv()
+        start_keys(d)
+    send_piece(1)
+    lax.fori_loop(2, 3, project, 0)
+    spread_piece(0)
     wait_relay(1)
     wait_relay(3)
     along_z(0, 2).wait_recv()
     start_keys(2)
+    lax.fori_loop(3, 4, project, 0)
+    key_rows = keys_out.at[pl.ds(pl.multiple_of(sec * ROWS, ROWS), ROWS)]
+    key_send = send(k_v, key_rows, keys_s, keys_r, partner)
+    key_send.start()
+    key_own = pltpu.make_async_copy(k_v, key_rows, own_sem.at[2, 0])
+    key_own.start()
+
     for d in (1, 3):
         along_z(1, d).wait_recv()
         start_queries(d)
+    spread_piece(1)
     wait_piece(y + 3, c, 0, wys.at[0], wyr.at[0])
     forward(y + 3, 0, wrs, wrr, 0, up)
     forward(y + 3, 0, wcs, wcr, 2, core)
@@ -345,7 +346,9 @@
         copy.wait_send()
 
 
-def spread(picked_k, picked_q, inputs, w_query, w_key, rope):
+def spread(picked_k, picked_q, inputs, w_query, w_key, order):
+    freqs = rope_base ** (-(np.arange(HD) % (HD // 2) * 2.0) / HD)
+    freqs = jnp.asarray(freqs.astype(np.float32)[None])
     return pl.pallas_call(
         spread_kernel,
         out_shape=(
@@ -354,11 +357,11 @@
             jax.ShapeDtypeStruct((2, 2, LEN, HD), BF16),
             jax.ShapeDtypeStruct((2, 2, ROWS, HD), BF16),
             jax.ShapeDtypeStruct((D, GW), BF16),
+            jax.ShapeDtypeStruct((2, ROWS, HD), F32),
         ),
-        in_specs=[ANY] * 6,
-        out_specs=(VMEM, ANY, ANY, ANY, ANY),
+        in_specs=[ANY] * 5 + [SMEM, VMEM],
+        out_specs=(VMEM, ANY, ANY, ANY, ANY, VMEM),
         scratch_shapes=[
-            pltpu.VMEM((2, ROWS, HD), F32),
             pltpu.VMEM((ROWS, D), BF16),
             pltpu.VMEM((D, GW), BF16),
             pltpu.VMEM((ROWS, HD), BF16),
@@ -382,13 +385,13 @@
             collective_id=1, has_side_effects=True, vmem_limit_bytes=63 * MIB
         ),
         name="spread",
-    )(picked_k, picked_q, inputs, w_query, w_key, rope)
+    )(picked_k, picked_q, inputs, w_query, w_key, order, freqs)
 
 
 def attend_kernel(
     order_ref, match_ref, q_ref, keys, gotq, gotk, rope,
     qg_ref, own_ref, other_ref,
-    kp, tkp, tqv, st, ms, g_acc, dk, sems, qsems,
+    q_t, t_t, k_t, kp, tkp, tqv, st, ms, g_acc, dk, sems, qsems,
 ):
     sec, head = lax.axis_index("sec"), lax.axis_index("head")
     exponent = scale * math.log2(math.e)
@@ -418,16 +421,20 @@
     for copy in copies:
         copy.wait()
 
-    nt = (((1,), (1,)), ((), ()))
-    tn = (((0,), (0,)), ((), ()))
+    for b in range(NBLK):
+        k_t[:, b * QB : (b + 1) * QB] = kp[b * QB : (b + 1) * QB, :].T
 
     def one_block(qb, _):
         rows = pl.ds(pl.multiple_of(qb * QB, QB), QB)
         block = order_ref[sec * HALF_BLKS + qb]
-        last = block // 2
+        last = block // 4
         queries = jnp.concatenate(
             [q_ref[rows, i * HD : (i + 1) * HD] for i in range(HEADS)], axis=0
         )
+
+        for i in range(HEADS):
+            q_t[:, i * HD : (i + 1) * HD] = q_ref[rows, i * HD : (i + 1) * HD].T
+            t_t[i] = tqv[i, rows, :].T
 
         def scores(chunk, carry, masked):
             at = pl.ds(pl.multiple_of(chunk * CK, CK), CK)
@@ -435,15 +442,11 @@
             for unit in range(6):
                 if unit < 2:
                     columns = slice(unit * 256, unit * 256 + 256)
-                    part = lax.dot_general(
-                        kp[at, :], queries[columns], nt, preferred_element_type=F32
-                    )
+                    part = jnp.dot(kp[at, :], q_t[:, columns], preferred_element_type=F32)
                 else:
                     i = unit - 2
                     columns = slice(QW + i * HD, QW + (i + 1) * HD)
-                    part = lax.dot_general(
-                        tkp[i, at, :], tqv[i, rows, :], nt, preferred_element_type=F32
-                    )
+                    part = jnp.dot(tkp[i, at, :], t_t[i], preferred_element_type=F32)
                 if masked:
                     key_at = lax.broadcasted_iota(jnp.int32, part.shape, 0) + chunk * CK
                     row_at = lax.broadcasted_iota(jnp.int32, part.shape, 1) % QB + block * QB
@@ -474,13 +477,13 @@
             g = both[:, :, :QW] * factor[None, :, :QW] - both[:, :, QW:] * factor[None, :, QW:]
             g = g.reshape(CK, QW).astype(BF16)
             dk[at, :] += jnp.dot(g, queries, preferred_element_type=F32)
-            g_acc[...] += lax.dot_general(g, kp[at, :], tn, preferred_element_type=F32)
+            g_acc[...] += jnp.dot(k_t[:, at], g, preferred_element_type=F32)
             return 0
 
         lax.fori_loop(0, last + 1, grads, 0)
         cosine, sine = rope[0, rows, :], rope[1, rows, :]
         for i in range(HEADS):
-            part = g_acc[i * QB : (i + 1) * QB, :] * scale
+            part = g_acc[:, i * QB : (i + 1) * QB].T * scale
             part = part * cosine - pltpu.roll(part, HD // 2, axis=1) * sine
             qg_ref[rows, i * HD : (i + 1) * HD] = part.astype(BF16)
         return 0
@@ -505,12 +508,15 @@
         in_specs=[SMEM, SMEM, VMEM, ANY, ANY, ANY, VMEM],
         out_specs=(VMEM, VMEM, VMEM),
         scratch_shapes=[
+            pltpu.VMEM((HD, QW), BF16),
+            pltpu.VMEM((HEADS, HD, QB), BF16),
+            pltpu.VMEM((HD, LEN), BF16),
             pltpu.VMEM((LEN, HD), BF16),
             pltpu.VMEM((HEADS, LEN, HD), BF16),
             pltpu.VMEM((HEADS, ROWS, HD), BF16),
             pltpu.VMEM((LEN, 2 * QW), F32),
             pltpu.VMEM((LEN // CK, 8, 2 * QW), F32),
-            pltpu.VMEM((QW, HD), F32),
+            pltpu.VMEM((HD, QW), F32),
             pltpu.VMEM((LEN, HD), F32),
             DMA((HEADS + 1, NBLK)),
             DMA((HEADS,)),
@@ -775,8 +781,10 @@
 
 
 def shards(inputs, w_query, w_key, teacher_queries, teacher_keys, head_match, block_order):
-    picked_k, picked_q, rope = pick(head_match, block_order, teacher_keys, teacher_queries)
-    queries, keys, gotk, gotq, w2 = spread(picked_k, picked_q, inputs, w_query, w_key, rope)
+    picked_k, picked_q = pick(head_match, teacher_keys, teacher_queries)
+    queries, keys, gotk, gotq, w2, rope = spread(
+        picked_k, picked_q, inputs, w_query, w_key, block_order
+    )
     query_grads, own, other = attend(block_order, head_match, queries, keys, gotq, gotk, rope)
     rows, grad_query, grad_key = finish(
         query_grads.reshape(4, 2, QB, QW), own, other, inputs, w_query, w_key, w2, rope

time: 167 us -> 162 us (0.970); the launches traced: 167 us -> 158 us
  Pallas kernels: 165 us -> 158 us
    pallas_call x1, Pallas kernels: 72.8 us -> 59.2 us  [finish(): pl.pallas_call(finish_kernel, out_shape=(jax.ShapeDtypeStruct((QB, D), BF...]
    pallas_call x1, Pallas kernels: 29 us -> 34.6 us  [attend(): pl.pallas_call(attend_kernel, out_shape=(jax.ShapeDtypeStruct((ROWS, QW),...]
    pallas_call x1, Pallas kernels: 55.7 us -> 58.2 us  [spread(): pl.pallas_call(spread_kernel, out_shape=(jax.ShapeDtypeStruct((ROWS, QW),...]
    pallas_call x1, Pallas kernels: 5.77 us -> 3.51 us  [pick(): pl.pallas_call(pick_kernel, out_shape=(jax.ShapeDtypeStruct(shape, BF16),...]
where the time goes in v3:
time: 162 us; the launch traced here: 158 us
  Pallas kernels  158 us (98%)
    pallas_call x1, Pallas kernels, finish(): pl.pallas_call(finish_kernel, out_shape=(jax.ShapeDtypeStruct((QB, D), BF...  59.2 us
    pallas_call x1, Pallas kernels, spread(): pl.pallas_call(spread_kernel, out_shape=(jax.ShapeDtypeStruct((ROWS, QW),...  58.2 us
    pallas_call x1, Pallas kernels, attend(): pl.pallas_call(attend_kernel, out_shape=(jax.ShapeDtypeStruct((ROWS, QW),...  34.6 us
    pallas_call x1, Pallas kernels, pick(): pl.pallas_call(pick_kernel, out_shape=(jax.ShapeDtypeStruct(shape, BF16),...  3.51 us

profile of v3, /device:TPU:0, one launch (start us, length us, event | category | flops | bytes accessed | tf_op | source)
XLA Modules:
  0.0 158.5 jit_solution(17659282762269520400)
XLA Ops:
  0.6 3.5 %pick.1 = (bf16[4,2,2,256,128]{4,3,2,1,0:T(8,128)(2,1)}, bf16[4,2,2,256,128]{4,3,2,1,0:T(8,128)(2,1)}) custom-call(s32[32]{0:T(128)} %match_ref.3, bf16[1,256,8192]{2,1,0:T(8,128)(2,1)} %tk_ref.1, bf16[1,256,8192]{2,1,0:T(8,128)(2,1)} %tq_ref.1), custom_call_target="tpu_custom_call" | custom-call | tf_op jit(solution)/shard_map/pick/pallas_call | solution.py:73
  4.2 58.2 %spread.1 = (bf16[1024,512]{1,0:T(8,128)(2,1)}, bf16[2048,128]{1,0:T(8,128)(2,1)}, bf16[2,2,2048,128]{3,2,1,0:T(8,128)(2,1)}, bf16[2,2,1024,128]{3,2,1,0:T(8,128...) custom-call(bf16[4,2,2,256,128]{4,3,2,1,0:T(8,128)(2,1)} %get-tuple-element.17.sk, ...), custom_call_target="tpu_custom_call" | custom-call | tf_op jit(solution)/shard_map/spread/pallas_call | solution.py:352
  62.3 34.6 %attend.1 = (bf16[1024,512]{1,0:T(8,128)(2,1)}, f32[1024,128]{1,0:T(8,128)}, bf16[1024,128]{1,0:T(8,128)(2,1)}) custom-call(s32[16]{0:T(128)} %order_ref.3, s32[32]{0:T(128)} %match_ref.3, bf16[1024,512]{1,0:T(8,128)(2,1)} %get-tuple-element.19.q_ref, bf16[2048,128]{1,0:T(8,128)(2,1)} %get-tuple-element.20.keys, ...), custom_call_target="tpu_custom_call" | custom-call | tf_op jit(solution)/shard_map/attend/pallas_call | solution.py:501
  97.0 59.2 %finish.1 = (bf16[128,4096]{1,0:T(8,128)(2,1)}, bf16[256,512]{1,0:T(8,128)(2,1)}, bf16[256,128]{1,0:T(8,128)(2,1)}) custom-call(bf16[4,2,128,512]{3,2,1,0:T(8,128)(2,1)} %bitcast.1, f32[1024,128]{1,0:T(8,128)} %get-tuple-element.25.own, bf16[1024,128]{1,0:T(8,128)(2,1)} %get-tuple-element.26.other, bf16[1,1024,4096]{2,1,0:T(8,128)(2,1)} %tok.3, ...), custom_call_target="tpu_custom_call" | custom-call | tf_op jit(solution)/shard_map/finish/pallas_call | solution.py:706
  156.2 2.1 %close.1 = (bf16[1,128,4096]{2,1,0:T(8,128)(2,1)}, bf16[256,512]{1,0:T(8,128)(2,1)}, bf16[256,128]{1,0:T(8,128)(2,1)}) custom-call(bf16[128,4096]{1,0:T(8,128)(2,1)} %get-tuple-element.28.rows, bf16[256,512]{1,0:T(8,128)(2,1)} %get-tuple-element.29.gq, bf16[256,128]{1,0:T(8,128)(2,1)} %get-tuple-element.30.gk), custom_call_target="tpu_custom_call" | custom-call | tf_op jit(solution)/shard_map/close/pallas_call | solution.py:768

commit v4 on v3

--- a/solution.py
+++ b/solution.py
@@ -389,8 +389,9 @@
 
 
 def attend_kernel(
-    order_ref, match_ref, q_ref, keys, gotq, gotk, rope,
+    order_ref, match_ref, q_in, keys, gotq, gotk, rope_in,
     qg_ref, own_ref, other_ref,
+    q_ref, rope,
     q_t, t_t, k_t, kp, tkp, tqv, st, ms, g_acc, dk, sems, qsems,
 ):
     sec, head = lax.axis_index("sec"), lax.axis_index("head")
@@ -403,26 +404,34 @@
         low = jnp.where(section == 0, lows[0], lows[1])
         slot = jnp.where(entry - section * TH_SEC == low, 0, 1)
         places.append((section, slot))
-    copies = []
+    copies, key_copies = [], []
+    for b in range(NBLK):
+        to = pl.ds(pl.multiple_of(order_ref[b] * QB, QB), QB)
+        at = pl.ds(b * QB, QB)
+        key_copies.append(pltpu.make_async_copy(keys.at[at], kp.at[to], sems.at[4, b]))
+        key_copies[-1].start()
+    copies.append(pltpu.make_async_copy(q_in, q_ref, qsems.at[4]))
+    copies[-1].start()
+    copies.append(pltpu.make_async_copy(rope_in, rope, qsems.at[5]))
+    copies[-1].start()
     for i, (section, slot) in enumerate(places):
         copies.append(pltpu.make_async_copy(gotq.at[section, slot], tqv.at[i], qsems.at[i]))
         copies[-1].start()
     for b in range(NBLK):
         to = pl.ds(pl.multiple_of(order_ref[b] * QB, QB), QB)
         at = pl.ds(b * QB, QB)
-        copies.append(pltpu.make_async_copy(keys.at[at], kp.at[to], sems.at[4, b]))
-        copies[-1].start()
         for i, (section, slot) in enumerate(places):
             copies.append(
                 pltpu.make_async_copy(gotk.at[section, slot, at], tkp.at[i, to], sems.at[i, b])
             )
             copies[-1].start()
     dk[...] = jnp.zeros_like(dk)
+    for copy in key_copies:
+        copy.wait()
+    for b in range(NBLK):
+        k_t[:, b * QB : (b + 1) * QB] = kp[b * QB : (b + 1) * QB, :].T
     for copy in copies:
         copy.wait()
-
-    for b in range(NBLK):
-        k_t[:, b * QB : (b + 1) * QB] = kp[b * QB : (b + 1) * QB, :].T
 
     def one_block(qb, _):
         rows = pl.ds(pl.multiple_of(qb * QB, QB), QB)
@@ -473,11 +482,17 @@
         def grads(chunk, _):
             at = pl.ds(pl.multiple_of(chunk * CK, CK), CK)
             factor = jnp.exp2((ms[chunk] - top) * exponent) * inverse
-            both = st[at, :].reshape(CK // 8, 8, 2 * QW)
-            g = both[:, :, :QW] * factor[None, :, :QW] - both[:, :, QW:] * factor[None, :, QW:]
-            g = g.reshape(CK, QW).astype(BF16)
-            dk[at, :] += jnp.dot(g, queries, preferred_element_type=F32)
-            g_acc[...] += jnp.dot(k_t[:, at], g, preferred_element_type=F32)
+            key_part = None
+            for pair in range(2):
+                student = slice(pair * 256, pair * 256 + 256)
+                teacher = slice(QW + pair * 256, QW + pair * 256 + 256)
+                p_s = st[at, student].reshape(CK // 8, 8, 256) * factor[None, :, student]
+                p_t = st[at, teacher].reshape(CK // 8, 8, 256) * factor[None, :, teacher]
+                g = (p_s - p_t).reshape(CK, 256).astype(BF16)
+                term = jnp.dot(g, queries[student], preferred_element_type=F32)
+                key_part = term if key_part is None else key_part + term
+                g_acc[:, student] += jnp.dot(k_t[:, at], g, preferred_element_type=F32)
+            dk[at, :] += key_part
             return 0
 
         lax.fori_loop(0, last + 1, grads, 0)
@@ -505,9 +520,11 @@
             jax.ShapeDtypeStruct((ROWS, HD), F32),
             jax.ShapeDtypeStruct((ROWS, HD), BF16),
         ),
-        in_specs=[SMEM, SMEM, VMEM, ANY, ANY, ANY, VMEM],
+        in_specs=[SMEM, SMEM, ANY, ANY, ANY, ANY, ANY],
         out_specs=(VMEM, VMEM, VMEM),
         scratch_shapes=[
+            pltpu.VMEM((ROWS, QW), BF16),
+            pltpu.VMEM((2, ROWS, HD), F32),
             pltpu.VMEM((HD, QW), BF16),
             pltpu.VMEM((HEADS, HD, QB), BF16),
             pltpu.VMEM((HD, LEN), BF16),
@@ -519,7 +536,7 @@
             pltpu.VMEM((HD, QW), F32),
             pltpu.VMEM((LEN, HD), F32),
             DMA((HEADS + 1, NBLK)),
-            DMA((HEADS,)),
+            DMA((HEADS + 2,)),
         ],
         compiler_params=pltpu.CompilerParams(vmem_limit_bytes=63 * MIB),
         name="attend",

time: 162 us -> 161 us (level)
    pallas_call x1, Pallas kernels: 59.2 us -> 61.7 us  [finish(): pl.pallas_call(finish_kernel, out_shape=(jax.ShapeDtypeStruct((QB, D), BF...]
    pallas_call x1, Pallas kernels: 34.6 us -> 32.3 us  [attend(): pl.pallas_call(attend_kernel, out_shape=(jax.ShapeDtypeStruct((ROWS, QW),...]
where the time goes in v4:
time: 161 us; the launch traced here: 159 us
  Pallas kernels  158 us (98%)
    pallas_call x1, Pallas kernels, finish(): pl.pallas_call(finish_kernel, out_shape=(jax.ShapeDtypeStruct((QB, D), BF...  61.7 us
    pallas_call x1, Pallas kernels, spread(): pl.pallas_call(spread_kernel, out_shape=(jax.ShapeDtypeStruct((ROWS, QW),...  58.1 us
    pallas_call x1, Pallas kernels, attend(): pl.pallas_call(attend_kernel, out_shape=(jax.ShapeDtypeStruct((ROWS, QW),...  32.3 us
    pallas_call x1, Pallas kernels, pick(): pl.pallas_call(pick_kernel, out_shape=(jax.ShapeDtypeStruct(shape, BF16),...  3.51 us

profile of v4, /device:TPU:0, one launch (start us, length us, event | category | flops | bytes accessed | tf_op | source)
XLA Modules:
  0.0 158.6 jit_solution(11923887722565658690)
XLA Ops:
  0.6 3.5 %pick.1 = (bf16[4,2,2,256,128]{4,3,2,1,0:T(8,128)(2,1)}, bf16[4,2,2,256,128]{4,3,2,1,0:T(8,128)(2,1)}) custom-call(s32[32]{0:T(128)} %match_ref.3, bf16[1,256,8192]{2,1,0:T(8,128)(2,1)} %tk_ref.1, bf16[1,256,8192]{2,1,0:T(8,128)(2,1)} %tq_ref.1), custom_call_target="tpu_custom_call" | custom-call | tf_op jit(solution)/shard_map/pick/pallas_call | solution.py:73
  4.2 58.1 %spread.1 = (bf16[1024,512]{1,0:T(8,128)(2,1)}, bf16[2048,128]{1,0:T(8,128)(2,1)}, bf16[2,2,2048,128]{3,2,1,0:T(8,128)(2,1)}, bf16[2,2,1024,128]{3,2,1,0:T(8,128...) custom-call(bf16[4,2,2,256,128]{4,3,2,1,0:T(8,128)(2,1)} %get-tuple-element.17.sk, ...), custom_call_target="tpu_custom_call" | custom-call | tf_op jit(solution)/shard_map/spread/pallas_call | solution.py:352
  62.3 32.3 %attend.1 = (bf16[1024,512]{1,0:T(8,128)(2,1)}, f32[1024,128]{1,0:T(8,128)}, bf16[1024,128]{1,0:T(8,128)(2,1)}) custom-call(s32[16]{0:T(128)} %order_ref.3, s32[32]{0:T(128)} %match_ref.3, bf16[1024,512]{1,0:T(8,128)(2,1)} %get-tuple-element.19.q_in, bf16[2048,128]{1,0:T(8,128)(2,1)} %get-tuple-element.20.keys, ...), custom_call_target="tpu_custom_call" | custom-call | tf_op jit(solution)/shard_map/attend/pallas_call | solution.py:516
  94.5 61.7 %finish.1 = (bf16[128,4096]{1,0:T(8,128)(2,1)}, bf16[256,512]{1,0:T(8,128)(2,1)}, bf16[256,128]{1,0:T(8,128)(2,1)}) custom-call(bf16[4,2,128,512]{3,2,1,0:T(8,128)(2,1)} %bitcast.1, f32[1024,128]{1,0:T(8,128)} %get-tuple-element.25.own, bf16[1024,128]{1,0:T(8,128)(2,1)} %get-tuple-element.26.other, bf16[1,1024,4096]{2,1,0:T(8,128)(2,1)} %tok.3, ...), custom_call_target="tpu_custom_call" | custom-call | tf_op jit(solution)/shard_map/finish/pallas_call | solution.py:723
  156.3 2.1 %close.1 = (bf16[1,128,4096]{2,1,0:T(8,128)(2,1)}, bf16[256,512]{1,0:T(8,128)(2,1)}, bf16[256,128]{1,0:T(8,128)(2,1)}) custom-call(bf16[128,4096]{1,0:T(8,128)(2,1)} %get-tuple-element.28.rows, bf16[256,512]{1,0:T(8,128)(2,1)} %get-tuple-element.29.gq, bf16[256,128]{1,0:T(8,128)(2,1)} %get-tuple-element.30.gk), custom_call_target="tpu_custom_call" | custom-call | tf_op jit(solution)/shard_map/close/pallas_call | solution.py:785
